TPU v7x, 32 devices: a whole 2x2x4 slice. The times are simulated.
32 devices in a mesh: gx: 16 (over z, y, core), gy: 2 (over x).
Axes of the slice: x: 2, y: 2, z: 4, core: 2. Of those that a mesh axis runs over, the one named last changes fastest.
Arguments:
- species: float32 [48, 128, 32, 128], P(None, 'gx', 'gy'), may hold values from 0.2 to 2
- rate_matrices: float32 [128, 32, 2304], P('gx', 'gy'), may hold values from -20 to 10, as said below
- loss_rates: float32 [48], replicated, may hold values from 0.05 to 0.5
- sweeps: int32 [128, 32], P('gx', 'gy'), may hold values from 5 to 10, as said below
- flow_rows: float32 [128, 32, 128], P('gx', 'gy'), may hold values from -0.24 to 0.24
- flow_columns: float32 [128, 32, 128], P('gx', 'gy'), may hold values from -0.24 to 0.24
Outputs:
- transported: float32 [48, 128, 32, 128], P(None, 'gx', 'gy')
Inputs may be any that keep to these rules, and one draw needn't show every extreme that they name: `rate_matrices`: each column's rate matrix times the time step, with a negative diagonal. Columns in rows 56 to 71 take 9 or 10 sweeps, all others 5 or 6; both 5 and 10 occur.
All inputs are finite; a program needn't handle non-finite values.
Results may differ from a plain program's by a relative error of at most 0.0003.
Values sent between devices are 32-bit elements; how exact they have to be, the bound alone decides.
A program may use at most 128 MiB of HBM per device.

v0:
```python
import jax
import jax.numpy as jnp
from jax import lax
from jax.sharding import PartitionSpec as P

section_gamma = 1.0 + 0.5**0.5


def from_behind(array, axis, by):
    length = lax.axis_size(axis)
    pairs = [(i, i + by) for i in range(length) if 0 <= i + by < length]
    return lax.ppermute(array, axis, pairs)


def padded_2(array, sides, width):
    for axis, dim in sides:
        size, length = (lax.axis_size(axis), array.shape[dim])
        up = [(i, (i + 1) % size) for i in range(size - 1)]
        down = [(j, i) for i, j in up]
        last = lax.slice_in_dim(array, length - width, length, axis=dim)
        first = lax.slice_in_dim(array, 0, width, axis=dim)
        before = lax.ppermute(last, axis, up)
        after = lax.ppermute(first, axis, down)
        array = jnp.concatenate([before, array, after], axis=dim)
    return array


def linear_parts(matrices):
    species_count = matrices.shape[-1]
    identity = jnp.eye(species_count, dtype=jnp.float32)
    diagonal = jnp.sum(matrices * identity, axis=-1)
    coupling = section_gamma * (matrices * (1.0 - identity))
    scaled = 1.0 - section_gamma * diagonal
    return (coupling, scaled)


def product(matrices, values):
    return jnp.einsum("bij,bjn->bin", matrices, values, precision=lax.Precision.HIGHEST)


def tendency(matrices, values, loss_rates):
    return product(matrices, values) - loss_rates[:, None] * values * values


def advect(concentration, flow_first, flow_second):
    row_flux = (
        jnp.maximum(flow_first[:-1], 0.0) * concentration[:, :-1]
        + jnp.minimum(flow_first[:-1], 0.0) * concentration[:, 1:]
    )
    column_flux = (
        jnp.maximum(flow_second[:, :-1], 0.0) * concentration[:, :, :-1]
        + jnp.minimum(flow_second[:, :-1], 0.0) * concentration[:, :, 1:]
    )
    interior = concentration[:, 1:-1, 1:-1]
    return (
        interior
        - (row_flux[:, 1:, 1:-1] - row_flux[:, :-1, 1:-1])
        - (column_flux[:, 1:-1, 1:] - column_flux[:, 1:-1, :-1])
    )


def react_blocks(values, matrices, counts, loss_rates):
    coupling, scaled = linear_parts(matrices)
    trip_count = jnp.max(counts)

    def run_sweeps(source):

        def sweep_once(sweep_index, solved):
            update = (source + product(coupling, solved)) / scaled[:, :, None]
            return jnp.where((sweep_index < counts)[:, None, None], update, solved)

        return lax.fori_loop(0, trip_count, sweep_once, jnp.zeros_like(source))

    section_one = run_sweeps(tendency(matrices, values, loss_rates))
    shifted = values + section_one
    second = run_sweeps(tendency(matrices, shifted, loss_rates) - 2.0 * section_one)
    return values + 1.5 * section_one + 0.5 * second


def on_device(species, rate_matrices, loss_rates, sweeps, flow_rows, flow_columns):
    species_count, rows_here, columns_here, depth = species.shape
    block_count = rows_here * columns_here
    columns_first = jnp.transpose(species, (1, 2, 0, 3)).reshape(block_count, species_count, depth)
    matrices = rate_matrices.reshape(block_count, species_count, species_count)
    counts = sweeps.reshape(block_count)
    reacted = react_blocks(columns_first, matrices, counts, loss_rates)
    concentration = jnp.transpose(
        reacted.reshape(rows_here, columns_here, species_count, depth), (2, 0, 1, 3)
    )
    below_rows = from_behind(flow_rows[-1:], "gx", 1)
    below_columns = from_behind(flow_columns[:, -1:], "gy", 1)
    empty_row = jnp.zeros_like(below_rows)
    empty_column = jnp.zeros_like(below_columns)
    first_wide = jnp.concatenate([below_rows, flow_rows, empty_row], 0)
    first_wide = jnp.pad(first_wide, ((0, 0), (1, 1), (0, 0)))
    second_wide = jnp.concatenate([below_columns, flow_columns, empty_column], 1)
    second_wide = jnp.pad(second_wide, ((1, 1), (0, 0), (0, 0)))
    transported = concentration
    for substep in range(2):
        padded = padded_2(transported, (("gx", 1), ("gy", 2)), 1)
        transported = advect(padded, first_wide, second_wide)
    return transported


def solution(mesh):
    placed = (
        P(None, "gx", "gy", None),
        P("gx", "gy", None),
        P(),
        P("gx", "gy"),
        P("gx", "gy", None),
        P("gx", "gy", None),
    )
    return jax.shard_map(
        on_device, mesh=mesh, in_specs=placed, out_specs=P(None, "gx", "gy", None), check_vma=False
    )
```

profile of v0, /device:TPU:12, one launch (start us, length us, event | category | flops | bytes accessed | tf_op | source)
XLA Modules:
  0.0 257.9 jit_solution(6631794937297303450)
XLA Ops:
  0.0 3.7 %copy.11 = f32[8,16,48,128]{3,2,1,0:T(8,128)S(1)} copy(f32[8,16,48,128]{3,1,0,2:T(8,128)} %bitcast.32) | data formatting | bytes 6291456 | tf_op jit(solution)/shard_map/transpose | solution.py:83
  3.8 4.6 %reshape.40 = f32[128,48,48]{2,1,0:T(8,128)} reshape(f32[8,16,2304]{2,1,0:T(8,128)} %param.11) | data formatting | bytes 2359296 | tf_op jit(solution)/shard_map/reshape | solution.py:84
  8.4 4.3 %multiply_reduce_fusion = (f32[128,48]{1,0:T(8,128)S(1)}, f32[128,48,48]{2,1,0:T(8,128)}) fusion(f32[128,48,48]{2,1,0:T(8,128)} %reshape.40, f32[48,48]{1,0:T(8,128)S(1)} %fusion.16, f32[48,48]{1,0:T(8,128)S(1)} %broadcast_subtract_fusion), kind=kLoop, calls=%fused_computation.32 | loop fusion | flops 1173504 | bytes 2402304 | tf_op jit(solution)/shard_map/reduce_sum | solution.py:31
  13.5 6.2 %fusion.4 = f32[128,48,128]{2,1,0:T(8,128)} fusion(f32[128,48,128]{2,1,0:T(8,128)S(1)} %bitcast.30, f32[128,48,48]{2,1,0:T(8,128)} %reshape.40, f32[48]{0:T(128)S(1)} %copy-done.8), kind=kOutput, calls=%fused_computation.20 | convolution fusion | flops 455344128 | bytes 7471296 | tf_op jit(solution)/shard_map/bij,bjn->bin/dot_general | solution.py:38
  19.9 45.4 %while.20 = (s32[]{:T(128)}, f32[128,48,128]{2,1,0:T(8,128)S(1)}, s32[]{:T(128)}, s32[128]{0:T(128)S(1)}, f32[128,48,48]{2,1,0:T(8,128)}, /*index=5*/f32[128,48,128]{2,1,0:T(8,128)}, f32[128,48]{1,0:T(8,128)S(1)}, s32[]{:T(128)}) while((s32[]{:T(128)}, f32[128,48,128]{2,1,0:T(8,128)S(1)}, s32[]{:T(128)}, s32[128]{0:T(128)S(1)}, ...), condition=%wide.region_3.4_spmd, body=%wide.region_2.3_spmd.sunk | while | flops 455344256 | bytes 34235280 | solution.py:72
  20.7 1.7 copy-done.1
  23.4 3.9 %divide_select_fusion.4 = f32[128,48,128]{2,1,0:T(8,128)S(1)} fusion(f32[128,48,128]{2,1,0:T(8,128)S(1)} %copy.30, f32[128,48,128]{2,1,0:T(8,128)S(1)} %copy-done.4, f32[128,48,48]{2,1,0:T(8,128)S(1)} %copy-done.1, f32[128,48]{1,0:T(8,128)S(1)} %get-tuple-element.235, pred[128]{0:T(512)(128)(4,1)S(1)} %broadcast_compare_fusion.4), kind=kOutput, calls=%fused_computation.clone.1 | convolution fusion | flops 455344128 | bytes 10641536 | tf_op jit(solution)/shard_map/while/body/bij,bjn->bin/dot_general | solution.py:38
  28.2 1.7 copy-done.1
  30.8 3.9 %divide_select_fusion.4 = f32[128,48,128]{2,1,0:T(8,128)S(1)} fusion(f32[128,48,128]{2,1,0:T(8,128)S(1)} %copy.30, f32[128,48,128]{2,1,0:T(8,128)S(1)} %copy-done.4, f32[128,48,48]{2,1,0:T(8,128)S(1)} %copy-done.1, f32[128,48]{1,0:T(8,128)S(1)} %get-tuple-element.235, pred[128]{0:T(512)(128)(4,1)S(1)} %broadcast_compare_fusion.4), kind=kOutput, calls=%fused_computation.clone.1 | convolution fusion | flops 455344128 | bytes 10641536 | tf_op jit(solution)/shard_map/while/body/bij,bjn->bin/dot_general | solution.py:38
  35.6 1.7 copy-done.1
  38.2 3.9 %divide_select_fusion.4 = f32[128,48,128]{2,1,0:T(8,128)S(1)} fusion(f32[128,48,128]{2,1,0:T(8,128)S(1)} %copy.30, f32[128,48,128]{2,1,0:T(8,128)S(1)} %copy-done.4, f32[128,48,48]{2,1,0:T(8,128)S(1)} %copy-done.1, f32[128,48]{1,0:T(8,128)S(1)} %get-tuple-element.235, pred[128]{0:T(512)(128)(4,1)S(1)} %broadcast_compare_fusion.4), kind=kOutput, calls=%fused_computation.clone.1 | convolution fusion | flops 455344128 | bytes 10641536 | tf_op jit(solution)/shard_map/while/body/bij,bjn->bin/dot_general | solution.py:38
  43.0 1.7 copy-done.1
  45.7 3.9 %divide_select_fusion.4 = f32[128,48,128]{2,1,0:T(8,128)S(1)} fusion(f32[128,48,128]{2,1,0:T(8,128)S(1)} %copy.30, f32[128,48,128]{2,1,0:T(8,128)S(1)} %copy-done.4, f32[128,48,48]{2,1,0:T(8,128)S(1)} %copy-done.1, f32[128,48]{1,0:T(8,128)S(1)} %get-tuple-element.235, pred[128]{0:T(512)(128)(4,1)S(1)} %broadcast_compare_fusion.4), kind=kOutput, calls=%fused_computation.clone.1 | convolution fusion | flops 455344128 | bytes 10641536 | tf_op jit(solution)/shard_map/while/body/bij,bjn->bin/dot_general | solution.py:38
  50.5 1.7 copy-done.1
  53.1 3.9 %divide_select_fusion.4 = f32[128,48,128]{2,1,0:T(8,128)S(1)} fusion(f32[128,48,128]{2,1,0:T(8,128)S(1)} %copy.30, f32[128,48,128]{2,1,0:T(8,128)S(1)} %copy-done.4, f32[128,48,48]{2,1,0:T(8,128)S(1)} %copy-done.1, f32[128,48]{1,0:T(8,128)S(1)} %get-tuple-element.235, pred[128]{0:T(512)(128)(4,1)S(1)} %broadcast_compare_fusion.4), kind=kOutput, calls=%fused_computation.clone.1 | convolution fusion | flops 455344128 | bytes 10641536 | tf_op jit(solution)/shard_map/while/body/bij,bjn->bin/dot_general | solution.py:38
  57.9 1.7 copy-done.1
  60.5 3.9 %divide_select_fusion.4 = f32[128,48,128]{2,1,0:T(8,128)S(1)} fusion(f32[128,48,128]{2,1,0:T(8,128)S(1)} %copy.30, f32[128,48,128]{2,1,0:T(8,128)S(1)} %copy-done.4, f32[128,48,48]{2,1,0:T(8,128)S(1)} %copy-done.1, f32[128,48]{1,0:T(8,128)S(1)} %get-tuple-element.235, pred[128]{0:T(512)(128)(4,1)S(1)} %broadcast_compare_fusion.4), kind=kOutput, calls=%fused_computation.clone.1 | convolution fusion | flops 455344128 | bytes 10641536 | tf_op jit(solution)/shard_map/while/body/bij,bjn->bin/dot_general | solution.py:38
  65.3 9.3 %fusion.6 = f32[128,48,128]{2,1,0:T(8,128)} fusion(f32[128,48,128]{2,1,0:T(8,128)S(1)} %get-tuple-element.81, f32[128,48,48]{2,1,0:T(8,128)} %reshape.40, f32[128,48,128]{2,1,0:T(8,128)} %bitcast.31, f32[48]{0:T(128)S(1)} %copy-done.8), kind=kOutput, calls=%fused_computation.22 | convolution fusion | flops 458489856 | bytes 10617024 | tf_op jit(solution)/shard_map/bij,bjn->bin/dot_general | solution.py:38
  74.6 1.9 broadcast.32
  76.4 57.7 %while.21 = (s32[]{:T(128)}, f32[128,48,128]{2,1,0:T(8,128)}, s32[]{:T(128)}, s32[128]{0:T(128)S(1)}, f32[128,48,48]{2,1,0:T(8,128)}, /*index=5*/f32[128,48,128]{2,1,0:T(8,128)}, f32[128,48]{1,0:T(8,128)S(1)}, s32[]{:T(128)}) while((s32[]{:T(128)}, f32[128,48,128]{2,1,0:T(8,128)}, s32[]{:T(128)}, s32[128]{0:T(128)S(1)}, ...), condition=%wide.region_5.6_spmd, body=%wide.region_4.5_spmd.sunk | while | flops 455344256 | bytes 34235280 | solution.py:72
  77.1 2.0 copy.31
  80.9 5.1 %divide_select_fusion.5 = f32[128,48,128]{2,1,0:T(8,128)} fusion(f32[128,48,128]{2,1,0:T(8,128)S(1)} %copy.31, f32[128,48,128]{2,1,0:T(8,128)S(1)} %copy-done.3, f32[128,48,48]{2,1,0:T(8,128)S(1)} %copy-done.2, f32[128,48]{1,0:T(8,128)S(1)} %get-tuple-element.259, pred[128]{0:T(512)(128)(4,1)S(1)} %broadcast_compare_fusion.5), kind=kOutput, calls=%fused_computation.2.clone.1 | convolution fusion | flops 455344128 | bytes 10641536 | tf_op jit(solution)/shard_map/while/body/bij,bjn->bin/dot_general | solution.py:38
  86.6 2.0 copy.31
  90.4 5.1 %divide_select_fusion.5 = f32[128,48,128]{2,1,0:T(8,128)} fusion(f32[128,48,128]{2,1,0:T(8,128)S(1)} %copy.31, f32[128,48,128]{2,1,0:T(8,128)S(1)} %copy-done.3, f32[128,48,48]{2,1,0:T(8,128)S(1)} %copy-done.2, f32[128,48]{1,0:T(8,128)S(1)} %get-tuple-element.259, pred[128]{0:T(512)(128)(4,1)S(1)} %broadcast_compare_fusion.5), kind=kOutput, calls=%fused_computation.2.clone.1 | convolution fusion | flops 455344128 | bytes 10641536 | tf_op jit(solution)/shard_map/while/body/bij,bjn->bin/dot_general | solution.py:38
  96.1 2.0 copy.31
  99.9 5.1 %divide_select_fusion.5 = f32[128,48,128]{2,1,0:T(8,128)} fusion(f32[128,48,128]{2,1,0:T(8,128)S(1)} %copy.31, f32[128,48,128]{2,1,0:T(8,128)S(1)} %copy-done.3, f32[128,48,48]{2,1,0:T(8,128)S(1)} %copy-done.2, f32[128,48]{1,0:T(8,128)S(1)} %get-tuple-element.259, pred[128]{0:T(512)(128)(4,1)S(1)} %broadcast_compare_fusion.5), kind=kOutput, calls=%fused_computation.2.clone.1 | convolution fusion | flops 455344128 | bytes 10641536 | tf_op jit(solution)/shard_map/while/body/bij,bjn->bin/dot_general | solution.py:38
  105.6 2.0 copy.31
  109.4 5.1 %divide_select_fusion.5 = f32[128,48,128]{2,1,0:T(8,128)} fusion(f32[128,48,128]{2,1,0:T(8,128)S(1)} %copy.31, f32[128,48,128]{2,1,0:T(8,128)S(1)} %copy-done.3, f32[128,48,48]{2,1,0:T(8,128)S(1)} %copy-done.2, f32[128,48]{1,0:T(8,128)S(1)} %get-tuple-element.259, pred[128]{0:T(512)(128)(4,1)S(1)} %broadcast_compare_fusion.5), kind=kOutput, calls=%fused_computation.2.clone.1 | convolution fusion | flops 455344128 | bytes 10641536 | tf_op jit(solution)/shard_map/while/body/bij,bjn->bin/dot_general | solution.py:38
  115.1 2.0 copy.31
  118.9 5.1 %divide_select_fusion.5 = f32[128,48,128]{2,1,0:T(8,128)} fusion(f32[128,48,128]{2,1,0:T(8,128)S(1)} %copy.31, f32[128,48,128]{2,1,0:T(8,128)S(1)} %copy-done.3, f32[128,48,48]{2,1,0:T(8,128)S(1)} %copy-done.2, f32[128,48]{1,0:T(8,128)S(1)} %get-tuple-element.259, pred[128]{0:T(512)(128)(4,1)S(1)} %broadcast_compare_fusion.5), kind=kOutput, calls=%fused_computation.2.clone.1 | convolution fusion | flops 455344128 | bytes 10641536 | tf_op jit(solution)/shard_map/while/body/bij,bjn->bin/dot_general | solution.py:38
  124.7 2.0 copy.31
  128.4 5.1 %divide_select_fusion.5 = f32[128,48,128]{2,1,0:T(8,128)} fusion(f32[128,48,128]{2,1,0:T(8,128)S(1)} %copy.31, f32[128,48,128]{2,1,0:T(8,128)S(1)} %copy-done.3, f32[128,48,48]{2,1,0:T(8,128)S(1)} %copy-done.2, f32[128,48]{1,0:T(8,128)S(1)} %get-tuple-element.259, pred[128]{0:T(512)(128)(4,1)S(1)} %broadcast_compare_fusion.5), kind=kOutput, calls=%fused_computation.2.clone.1 | convolution fusion | flops 455344128 | bytes 10641536 | tf_op jit(solution)/shard_map/while/body/bij,bjn->bin/dot_general | solution.py:38
  134.1 3.5 %multiply_add_fusion = f32[128,48,128]{2,1,0:T(8,128)S(1)} fusion(f32[128,48,128]{2,1,0:T(8,128)} %get-tuple-element.82, f32[128,48,128]{2,1,0:T(8,128)S(1)} %get-tuple-element.81, f32[8,16,48,128]{3,2,1,0:T(8,128)} %copy-done), kind=kLoop, calls=%fused_computation.31 | loop fusion | flops 3145728 | bytes 12582912 | tf_op jit(solution)/shard_map/add | solution.py:77
  137.7 69.5 %collective-permute-start.1 = (f32[48,1,16,128]{3,0,2,1:T(8,128)S(1)}, f32[48,1,16,128]{3,0,2,1:T(8,128)S(1)}, u32[]{:S(2)}, u32[]{:S(2)}) collective-permute-start(f32[48,1,16,128]{3,0,2,1:T(8,128)S(1)} %get-tuple-element.117), channel_id=1, source_target_pairs={{0,2},{2,4},{4,6},{6,8},{8,10},{10,12},{12,14},{14,16},{16,18},{18... | collective-permute-start | bytes 1179656 | tf_op jit(solution)/shard_map/ppermute | solution.py:22
  207.2 1.9 collective-permute-start.2
  209.2 3.4 %collective-permute-start.5 = (f32[8,1,128]{2,1,0:T(1,128)S(1)}, f32[8,1,128]{2,1,0:T(1,128)S(1)}, u32[]{:S(2)}, u32[]{:S(2)}) collective-permute-start(f32[8,1,128]{2,1,0:T(1,128)S(1)} %slice.96), channel_id=1, source_target_pairs={{0,1},{2,3},{4,5},{6,7},{8,9},{10,11},{12,13},{14,15},{16,17},{18,... | collective-permute-start | bytes 12296 | tf_op jit(solution)/shard_map/ppermute | solution.py:12
  212.6 3.4 %collective-permute-start = (f32[1,16,128]{2,1,0:T(8,128)S(1)}, f32[1,16,128]{2,1,0:T(8,128)S(1)}, u32[]{:S(2)}, u32[]{:S(2)}) collective-permute-start(f32[1,16,128]{2,1,0:T(8,128)S(1)} %slice.86), channel_id=1, source_target_pairs={{0,2},{2,4},{4,6},{6,8},{8,10},{10,12},{12,14},{14,16},{16,18},{18... | collective-permute-start | bytes 24584 | tf_op jit(solution)/shard_map/ppermute | solution.py:12
  216.3 1.9 collective-permute-start.3
  219.7 2.3 collective-permute-done.3
  221.9 4.4 %collective-permute-done.4 = f32[48,10,1,128]{3,0,2,1:T(8,128)S(1)} collective-permute-done((f32[48,10,1,128]{3,0,2,1:T(8,128)S(1)}, f32[48,10,1,128]{3,0,2,1:T(8,128)S(1)}, u32[]{:S(2)}, u32[]{:S(2)}) %collective-permute-start.4) | collective-permute-done | bytes 245792 | tf_op jit(solution)/shard_map/ppermute | solution.py:23
  229.7 4.8 %collective-permute-start.6 = (f32[48,1,16,128]{3,0,2,1:T(8,128)S(1)}, f32[48,1,16,128]{3,0,2,1:T(8,128)S(1)}, u32[]{:S(2)}, u32[]{:S(2)}) collective-permute-start(f32[48,1,16,128]{3,0,2,1:T(8,128)S(1)} %get-tuple-element.115), channel_id=1, source_target_pairs={{0,2},{2,4},{4,6},{6,8},{8,10},{10,12},{12,14},{14,16},{16,18},{18... | collective-permute-start | bytes 1179656 | tf_op jit(solution)/shard_map/ppermute | solution.py:22
  234.5 1.9 collective-permute-start.7
  236.4 2.4 collective-permute-done.6
  238.8 2.9 %collective-permute-done.7 = f32[48,1,16,128]{3,0,2,1:T(8,128)S(1)} collective-permute-done((f32[48,1,16,128]{3,0,2,1:T(8,128)S(1)}, f32[48,1,16,128]{3,0,2,1:T(8,128)S(1)}, u32[]{:S(2)}, u32[]{:S(2)}) %collective-permute-start.7) | collective-permute-done | bytes 393248 | tf_op jit(solution)/shard_map/ppermute | solution.py:23
  241.7 1.8 collective-permute-start.8
  245.0 2.2 collective-permute-done.8
  247.2 4.4 %collective-permute-done.9 = f32[48,10,1,128]{3,0,2,1:T(8,128)S(1)} collective-permute-done((f32[48,10,1,128]{3,0,2,1:T(8,128)S(1)}, f32[48,10,1,128]{3,0,2,1:T(8,128)S(1)}, u32[]{:S(2)}, u32[]{:S(2)}) %collective-permute-start.9) | collective-permute-done | bytes 245792 | tf_op jit(solution)/shard_map/ppermute | solution.py:23
  255.2 2.6 %copy.12 = f32[48,8,16,128]{3,2,1,0:T(8,128)} copy(f32[48,8,16,128]{3,0,2,1:T(8,128)S(1)} %fusion.7) | data formatting | bytes 6291456 | tf_op jit(solution)/shard_map/sub | solution.py:56
  (102 shorter events, 28.7 us)
Async XLA Ops:
  3.7 15.9 %copy-start = (f32[8,16,48,128]{3,2,1,0:T(8,128)}, f32[8,16,48,128]{3,2,1,0:T(8,128)S(1)}, u32[]{:S(2)}) copy-start(f32[8,16,48,128]{3,2,1,0:T(8,128)S(1)} %copy.11) | copy-start | bytes 9437188
  8.4 4.4 %copy-start.7 = (s32[8,16]{1,0:T(8,128)S(1)}, s32[8,16]{1,0:T(8,128)}, u32[]{:S(2)}) copy-start(s32[8,16]{1,0:T(8,128)} %param.13) | copy-start | bytes 1540
  8.4 5.1 %copy-start.8 = (f32[48]{0:T(128)S(1)}, f32[48]{0:T(128)}, u32[]{:S(2)}) copy-start(f32[48]{0:T(128)} %param.12) | copy-start | bytes 580
  20.5 1.9 copy-start.1
  20.5 2.8 %copy-start.4 = (f32[128,48,128]{2,1,0:T(8,128)S(1)}, f32[128,48,128]{2,1,0:T(8,128)}, u32[]{:S(2)}) copy-start(f32[128,48,128]{2,1,0:T(8,128)} %get-tuple-element.234) | copy-start | bytes 9437188 | tf_op jit(solution)/shard_map/while
  27.9 1.9 copy-start.1
  27.9 2.8 %copy-start.4 = (f32[128,48,128]{2,1,0:T(8,128)S(1)}, f32[128,48,128]{2,1,0:T(8,128)}, u32[]{:S(2)}) copy-start(f32[128,48,128]{2,1,0:T(8,128)} %get-tuple-element.234) | copy-start | bytes 9437188 | tf_op jit(solution)/shard_map/while
  35.4 1.9 copy-start.1
  35.4 2.8 %copy-start.4 = (f32[128,48,128]{2,1,0:T(8,128)S(1)}, f32[128,48,128]{2,1,0:T(8,128)}, u32[]{:S(2)}) copy-start(f32[128,48,128]{2,1,0:T(8,128)} %get-tuple-element.234) | copy-start | bytes 9437188 | tf_op jit(solution)/shard_map/while
  42.8 1.9 copy-start.1
  42.8 2.8 %copy-start.4 = (f32[128,48,128]{2,1,0:T(8,128)S(1)}, f32[128,48,128]{2,1,0:T(8,128)}, u32[]{:S(2)}) copy-start(f32[128,48,128]{2,1,0:T(8,128)} %get-tuple-element.234) | copy-start | bytes 9437188 | tf_op jit(solution)/shard_map/while
  50.2 1.9 copy-start.1
  50.3 2.8 %copy-start.4 = (f32[128,48,128]{2,1,0:T(8,128)S(1)}, f32[128,48,128]{2,1,0:T(8,128)}, u32[]{:S(2)}) copy-start(f32[128,48,128]{2,1,0:T(8,128)} %get-tuple-element.234) | copy-start | bytes 9437188 | tf_op jit(solution)/shard_map/while
  57.7 1.9 copy-start.1
  57.7 2.8 %copy-start.4 = (f32[128,48,128]{2,1,0:T(8,128)S(1)}, f32[128,48,128]{2,1,0:T(8,128)}, u32[]{:S(2)}) copy-start(f32[128,48,128]{2,1,0:T(8,128)} %get-tuple-element.234) | copy-start | bytes 9437188 | tf_op jit(solution)/shard_map/while
  77.1 2.8 %copy-start.2 = (f32[128,48,48]{2,1,0:T(8,128)S(1)}, f32[128,48,48]{2,1,0:T(8,128)}, u32[]{:S(2)}) copy-start(f32[128,48,48]{2,1,0:T(8,128)} %get-tuple-element.257) | copy-start | bytes 3538948 | tf_op jit(solution)/shard_map/while
  77.1 3.8 %copy-start.3 = (f32[128,48,128]{2,1,0:T(8,128)S(1)}, f32[128,48,128]{2,1,0:T(8,128)}, u32[]{:S(2)}) copy-start(f32[128,48,128]{2,1,0:T(8,128)} %get-tuple-element.258) | copy-start | bytes 9437188 | tf_op jit(solution)/shard_map/while
  86.6 2.8 %copy-start.2 = (f32[128,48,48]{2,1,0:T(8,128)S(1)}, f32[128,48,48]{2,1,0:T(8,128)}, u32[]{:S(2)}) copy-start(f32[128,48,48]{2,1,0:T(8,128)} %get-tuple-element.257) | copy-start | bytes 3538948 | tf_op jit(solution)/shard_map/while
  86.6 3.8 %copy-start.3 = (f32[128,48,128]{2,1,0:T(8,128)S(1)}, f32[128,48,128]{2,1,0:T(8,128)}, u32[]{:S(2)}) copy-start(f32[128,48,128]{2,1,0:T(8,128)} %get-tuple-element.258) | copy-start | bytes 9437188 | tf_op jit(solution)/shard_map/while
  96.1 2.8 %copy-start.2 = (f32[128,48,48]{2,1,0:T(8,128)S(1)}, f32[128,48,48]{2,1,0:T(8,128)}, u32[]{:S(2)}) copy-start(f32[128,48,48]{2,1,0:T(8,128)} %get-tuple-element.257) | copy-start | bytes 3538948 | tf_op jit(solution)/shard_map/while
  96.1 3.8 %copy-start.3 = (f32[128,48,128]{2,1,0:T(8,128)S(1)}, f32[128,48,128]{2,1,0:T(8,128)}, u32[]{:S(2)}) copy-start(f32[128,48,128]{2,1,0:T(8,128)} %get-tuple-element.258) | copy-start | bytes 9437188 | tf_op jit(solution)/shard_map/while
  105.6 2.8 %copy-start.2 = (f32[128,48,48]{2,1,0:T(8,128)S(1)}, f32[128,48,48]{2,1,0:T(8,128)}, u32[]{:S(2)}) copy-start(f32[128,48,48]{2,1,0:T(8,128)} %get-tuple-element.257) | copy-start | bytes 3538948 | tf_op jit(solution)/shard_map/while
  105.6 3.8 %copy-start.3 = (f32[128,48,128]{2,1,0:T(8,128)S(1)}, f32[128,48,128]{2,1,0:T(8,128)}, u32[]{:S(2)}) copy-start(f32[128,48,128]{2,1,0:T(8,128)} %get-tuple-element.258) | copy-start | bytes 9437188 | tf_op jit(solution)/shard_map/while
  115.1 2.8 %copy-start.2 = (f32[128,48,48]{2,1,0:T(8,128)S(1)}, f32[128,48,48]{2,1,0:T(8,128)}, u32[]{:S(2)}) copy-start(f32[128,48,48]{2,1,0:T(8,128)} %get-tuple-element.257) | copy-start | bytes 3538948 | tf_op jit(solution)/shard_map/while
  115.1 3.8 %copy-start.3 = (f32[128,48,128]{2,1,0:T(8,128)S(1)}, f32[128,48,128]{2,1,0:T(8,128)}, u32[]{:S(2)}) copy-start(f32[128,48,128]{2,1,0:T(8,128)} %get-tuple-element.258) | copy-start | bytes 9437188 | tf_op jit(solution)/shard_map/while
  124.6 2.8 %copy-start.2 = (f32[128,48,48]{2,1,0:T(8,128)S(1)}, f32[128,48,48]{2,1,0:T(8,128)}, u32[]{:S(2)}) copy-start(f32[128,48,48]{2,1,0:T(8,128)} %get-tuple-element.257) | copy-start | bytes 3538948 | tf_op jit(solution)/shard_map/while
  124.6 3.8 %copy-start.3 = (f32[128,48,128]{2,1,0:T(8,128)S(1)}, f32[128,48,128]{2,1,0:T(8,128)}, u32[]{:S(2)}) copy-start(f32[128,48,128]{2,1,0:T(8,128)} %get-tuple-element.258) | copy-start | bytes 9437188 | tf_op jit(solution)/shard_map/while
  134.1 75.0 %copy-start.6 = (f32[8,16,128]{2,1,0:T(8,128)S(1)}, f32[8,16,128]{2,1,0:T(8,128)}, u32[]{:S(2)}) copy-start(f32[8,16,128]{2,1,0:T(8,128)} %param.15) | copy-start | bytes 196612
  134.1 78.4 %copy-start.5 = (f32[8,16,128]{2,1,0:T(8,128)S(1)}, f32[8,16,128]{2,1,0:T(8,128)}, u32[]{:S(2)}) copy-start(f32[8,16,128]{2,1,0:T(8,128)} %param.14) | copy-start | bytes 196612
  137.7 78.6 %collective-permute-start.1 = (f32[48,1,16,128]{3,0,2,1:T(8,128)S(1)}, f32[48,1,16,128]{3,0,2,1:T(8,128)S(1)}, u32[]{:S(2)}, u32[]{:S(2)}) collective-permute-start(f32[48,1,16,128]{3,0,2,1:T(8,128)S(1)} %get-tuple-element.117), channel_id=1, source_target_pairs={{0,2},{2,4},{4,6},{6,8},{8,10},{10,12},{12,14},{14,16},{16,18},{18... | collective-permute-start | bytes 1179656 | tf_op jit(solution)/shard_map/ppermute | solution.py:22
  207.2 9.1 %collective-permute-start.2 = (f32[48,1,16,128]{3,0,2,1:T(8,128)S(1)}, f32[48,1,16,128]{3,0,2,1:T(8,128)S(1)}, u32[]{:S(2)}, u32[]{:S(2)}) collective-permute-start(f32[48,1,16,128]{3,0,2,1:T(8,128)S(1)} %get-tuple-element.118), channel_id=1, source_target_pairs={{2,0},{4,2},{6,4},{8,6},{10,8},{12,10},{14,12},{16,14},{18,16},{20... | collective-permute-start | bytes 1179656 | tf_op jit(solution)/shard_map/ppermute | solution.py:23
  209.2 7.0 %collective-permute-start.5 = (f32[8,1,128]{2,1,0:T(1,128)S(1)}, f32[8,1,128]{2,1,0:T(1,128)S(1)}, u32[]{:S(2)}, u32[]{:S(2)}) collective-permute-start(f32[8,1,128]{2,1,0:T(1,128)S(1)} %slice.96), channel_id=1, source_target_pairs={{0,1},{2,3},{4,5},{6,7},{8,9},{10,11},{12,13},{14,15},{16,17},{18,... | collective-permute-start | bytes 12296 | tf_op jit(solution)/shard_map/ppermute | solution.py:12
  212.6 7.0 %collective-permute-start = (f32[1,16,128]{2,1,0:T(8,128)S(1)}, f32[1,16,128]{2,1,0:T(8,128)S(1)}, u32[]{:S(2)}, u32[]{:S(2)}) collective-permute-start(f32[1,16,128]{2,1,0:T(8,128)S(1)} %slice.86), channel_id=1, source_target_pairs={{0,2},{2,4},{4,6},{6,8},{8,10},{10,12},{12,14},{14,16},{16,18},{18... | collective-permute-start | bytes 24584 | tf_op jit(solution)/shard_map/ppermute | solution.py:12
  216.3 5.6 %collective-permute-start.3 = (f32[48,10,1,128]{3,0,2,1:T(8,128)S(1)}, f32[48,10,1,128]{3,0,2,1:T(8,128)S(1)}, u32[]{:S(2)}, u32[]{:S(2)}) collective-permute-start(f32[48,10,1,128]{3,0,2,1:T(8,128)S(1)} %get-tuple-element.114), channel_id=1, source_target_pairs={{0,1},{2,3},{4,5},{6,7},{8,9},{10,11},{12,13},{14,15},{16,17},{18,... | collective-permute-start | bytes 737288 | tf_op jit(solution)/shard_map/ppermute | solution.py:22
  218.3 8.1 %collective-permute-start.4 = (f32[48,10,1,128]{3,0,2,1:T(8,128)S(1)}, f32[48,10,1,128]{3,0,2,1:T(8,128)S(1)}, u32[]{:S(2)}, u32[]{:S(2)}) collective-permute-start(f32[48,10,1,128]{3,0,2,1:T(8,128)S(1)} %get-tuple-element.113), channel_id=1, source_target_pairs={{1,0},{3,2},{5,4},{7,6},{9,8},{11,10},{13,12},{15,14},{17,16},{19,... | collective-permute-start | bytes 737288 | tf_op jit(solution)/shard_map/ppermute | solution.py:23
  229.7 9.1 %collective-permute-start.6 = (f32[48,1,16,128]{3,0,2,1:T(8,128)S(1)}, f32[48,1,16,128]{3,0,2,1:T(8,128)S(1)}, u32[]{:S(2)}, u32[]{:S(2)}) collective-permute-start(f32[48,1,16,128]{3,0,2,1:T(8,128)S(1)} %get-tuple-element.115), channel_id=1, source_target_pairs={{0,2},{2,4},{4,6},{6,8},{8,10},{10,12},{12,14},{14,16},{16,18},{18... | collective-permute-start | bytes 1179656 | tf_op jit(solution)/shard_map/ppermute | solution.py:22
  234.5 7.2 %collective-permute-start.7 = (f32[48,1,16,128]{3,0,2,1:T(8,128)S(1)}, f32[48,1,16,128]{3,0,2,1:T(8,128)S(1)}, u32[]{:S(2)}, u32[]{:S(2)}) collective-permute-start(f32[48,1,16,128]{3,0,2,1:T(8,128)S(1)} %get-tuple-element.116), channel_id=1, source_target_pairs={{2,0},{4,2},{6,4},{8,6},{10,8},{12,10},{14,12},{16,14},{18,16},{20... | collective-permute-start | bytes 1179656 | tf_op jit(solution)/shard_map/ppermute | solution.py:23
  241.7 5.4 %collective-permute-start.8 = (f32[48,10,1,128]{3,0,2,1:T(8,128)S(1)}, f32[48,10,1,128]{3,0,2,1:T(8,128)S(1)}, u32[]{:S(2)}, u32[]{:S(2)}) collective-permute-start(f32[48,10,1,128]{3,0,2,1:T(8,128)S(1)} %get-tuple-element.112), channel_id=1, source_target_pairs={{0,1},{2,3},{4,5},{6,7},{8,9},{10,11},{12,13},{14,15},{16,17},{18,... | collective-permute-start | bytes 737288 | tf_op jit(solution)/shard_map/ppermute | solution.py:22
  243.5 8.1 %collective-permute-start.9 = (f32[48,10,1,128]{3,0,2,1:T(8,128)S(1)}, f32[48,10,1,128]{3,0,2,1:T(8,128)S(1)}, u32[]{:S(2)}, u32[]{:S(2)}) collective-permute-start(f32[48,10,1,128]{3,0,2,1:T(8,128)S(1)} %get-tuple-element.111), channel_id=1, source_target_pairs={{1,0},{3,2},{5,4},{7,6},{9,8},{11,10},{13,12},{15,14},{17,16},{19,... | collective-permute-start | bytes 737288 | tf_op jit(solution)/shard_map/ppermute | solution.py:23
where the time goes:
time: 261 us; the launch traced here: 258 us
  starting transfers between devices  91.4 us (35%)
  matrix products  69.5 us (27%)
  local copies, waits for them, and re-layouts  53 us (20%)
  waiting for transfers between devices  18.5 us (7%)
  other arithmetic  15.7 us (6%)
  loops' own time  9.35 us (4%)
    ppermute x4, starting transfers between devices, padded_2(): before = lax.ppermute(last, axis, up)  78 us
    dot_general x14, matrix products, product(): jnp.einsum('bij,bjn->bin', matrices, values, precision=lax.Precision.HIGH...  69.5 us
    while x60, local copies, waits for them, and re-layouts  39.6 us
    ppermute x4, waiting for transfers between devices, padded_2(): after = lax.ppermute(first, axis, down)  11.7 us
    another operation x2, loops' own time, run_sweeps(): return lax.fori_loop(0, trip_count, sweep_once, jnp.zeros_like(source))  9.35 us
    ppermute x2, starting transfers between devices, from_behind(): return lax.ppermute(array, axis, pairs)  6.82 us
    ppermute x4, waiting for transfers between devices, padded_2(): before = lax.ppermute(last, axis, up)  6.81 us
    ppermute x4, starting transfers between devices, padded_2(): after = lax.ppermute(first, axis, down)  6.65 us
  transfers between devices with their start and end apart: 10, of which 6 were waited for; matrix products, arithmetic and copies ran while one was open for 0% of the time, Pallas kernels for 0%

commit v1 on v0

v1 whole, which is shorter than its diff:
```python
import jax
import jax.numpy as jnp
from jax import lax
from jax.experimental import pallas as pl
from jax.experimental.pallas import tpu as pltpu
from jax.sharding import PartitionSpec as P

section_gamma = 1.0 + 0.5**0.5


def halves(x):
    hi = x.astype(jnp.bfloat16)
    return hi, (x - hi.astype(jnp.float32)).astype(jnp.bfloat16)


def left(x):
    hi, lo = halves(x)
    return jnp.concatenate([hi, lo, hi], axis=1)


def right(x):
    hi, lo = halves(x)
    return jnp.concatenate([hi, hi, lo], axis=0)


def mm(a, b):
    return jnp.dot(a, b, preferred_element_type=jnp.float32)


def react(matrix, v, count, loss, eye):
    diagonal = jnp.sum(jnp.where(eye, matrix, 0.0), axis=1, keepdims=True)
    inverse = 1.0 / (1.0 - section_gamma * diagonal)
    m1 = jnp.where(eye, 0.0, matrix * (section_gamma * inverse))
    right_1 = right(m1)
    m2 = mm(left(m1), right_1)
    left_2 = left(m2)
    m3 = mm(left_2, right_1)
    m4 = mm(left_2, right(m2))
    left_4 = left(m4)
    m5 = mm(left_4, right_1)
    p4 = jnp.where(eye, 1.0, 0.0) + m1 + m2 + m3
    even = jnp.where(count % 2 == 0, 1.0, 0.0)
    short = p4 + m4 + even * m5
    full = p4 + mm(left_4, right(short))
    left_p = left(jnp.where(count > 8, full, short))
    left_a = left(matrix)
    r1 = mm(left_a, right(v)) - loss * v * v
    k1 = mm(left_p, right(r1 * inverse))
    w = v + k1
    r2 = mm(left_a, right(w)) - loss * w * w - 2.0 * k1
    k2 = mm(left_p, right(r2 * inverse))
    return v + 1.5 * k1 + 0.5 * k2


def reaction_kernel(species_ref, rates_ref, loss_ref, sweeps_ref, out_ref, rows_ref):
    count, nx, ny, depth = species_ref.shape
    flat = species_ref.reshape(count * nx * ny, depth)
    eye = lax.broadcasted_iota(jnp.int32, (count, count), 0) == lax.broadcasted_iota(
        jnp.int32, (count, count), 1
    )
    loss = jnp.sum(jnp.where(eye, loss_ref[...], 0.0), axis=1, keepdims=True)
    halves_of_row = ny // 8

    @pl.loop(0, nx * halves_of_row)
    def _(octet):
        x = octet // halves_of_row
        first = pl.multiple_of((octet % halves_of_row) * 8, 8)
        for i in range(count):
            rows_ref[i * 8 : i * 8 + 8, 0:count] = rates_ref[
                x, pl.ds(first, 8), i * count : (i + 1) * count
            ]
        for j in range(8):
            y = first + j
            matrix = rows_ref[pl.ds(j, count, stride=8), :][:, :count]
            v = flat[pl.ds(x * ny + y, count, stride=nx * ny), :]
            out_ref[x, y] = react(matrix, v, sweeps_ref[x, y], loss, eye)


def reaction(species, rates, loss, sweeps):
    count, nx, ny, depth = species.shape
    vmem = pl.BlockSpec(memory_space=pltpu.VMEM)
    return pl.pallas_call(
        reaction_kernel,
        out_shape=jax.ShapeDtypeStruct((nx, ny, count, depth), jnp.float32),
        in_specs=[vmem, vmem, vmem, pl.BlockSpec(memory_space=pltpu.SMEM)],
        out_specs=vmem,
        scratch_shapes=[pltpu.VMEM((count * 8, 128), jnp.float32)],
        compiler_params=pltpu.CompilerParams(vmem_limit_bytes=40 * 2**20),
        name="reaction",
    )(species, rates, loss.reshape(1, count), sweeps)


def from_behind(array, axis, by):
    length = lax.axis_size(axis)
    pairs = [(i, i + by) for i in range(length) if 0 <= i + by < length]
    return lax.ppermute(array, axis, pairs)


def padded_2(array, sides, width):
    for axis, dim in sides:
        size, length = (lax.axis_size(axis), array.shape[dim])
        up = [(i, (i + 1) % size) for i in range(size - 1)]
        down = [(j, i) for i, j in up]
        last = lax.slice_in_dim(array, length - width, length, axis=dim)
        first = lax.slice_in_dim(array, 0, width, axis=dim)
        before = lax.ppermute(last, axis, up)
        after = lax.ppermute(first, axis, down)
        array = jnp.concatenate([before, array, after], axis=dim)
    return array


def advect(concentration, flow_first, flow_second):
    row_flux = (
        jnp.maximum(flow_first[:-1], 0.0) * concentration[:, :-1]
        + jnp.minimum(flow_first[:-1], 0.0) * concentration[:, 1:]
    )
    column_flux = (
        jnp.maximum(flow_second[:, :-1], 0.0) * concentration[:, :, :-1]
        + jnp.minimum(flow_second[:, :-1], 0.0) * concentration[:, :, 1:]
    )
    interior = concentration[:, 1:-1, 1:-1]
    return (
        interior
        - (row_flux[:, 1:, 1:-1] - row_flux[:, :-1, 1:-1])
        - (column_flux[:, 1:-1, 1:] - column_flux[:, 1:-1, :-1])
    )


def on_device(species, rate_matrices, loss_rates, sweeps, flow_rows, flow_columns):
    reacted = reaction(species, rate_matrices, loss_rates, sweeps)
    concentration = jnp.transpose(reacted, (2, 0, 1, 3))
    below_rows = from_behind(flow_rows[-1:], "gx", 1)
    below_columns = from_behind(flow_columns[:, -1:], "gy", 1)
    empty_row = jnp.zeros_like(below_rows)
    empty_column = jnp.zeros_like(below_columns)
    first_wide = jnp.concatenate([below_rows, flow_rows, empty_row], 0)
    first_wide = jnp.pad(first_wide, ((0, 0), (1, 1), (0, 0)))
    second_wide = jnp.concatenate([below_columns, flow_columns, empty_column], 1)
    second_wide = jnp.pad(second_wide, ((1, 1), (0, 0), (0, 0)))
    transported = concentration
    for substep in range(2):
        padded = padded_2(transported, (("gx", 1), ("gy", 2)), 1)
        transported = advect(padded, first_wide, second_wide)
    return transported


def solution(mesh):
    placed = (
        P(None, "gx", "gy", None),
        P("gx", "gy", None),
        P(),
        P("gx", "gy"),
        P("gx", "gy", None),
        P("gx", "gy", None),
    )
    return jax.shard_map(
        on_device, mesh=mesh, in_specs=placed, out_specs=P(None, "gx", "gy", None), check_vma=False
    )
```

time: 261 us -> 184 us (0.70); the launches traced: 258 us -> 184 us
  Pallas kernels: 0 us -> 120 us
  matrix products: 69.5 us -> 0 us
  starting transfers between devices: 91.4 us -> 24 us
  local copies, waits for them, and re-layouts: 53 us -> 7.4 us
  loops' own time: 9.35 us -> 0 us
  other arithmetic: 15.7 us -> 6.72 us
  waiting for transfers between devices: 18.5 us -> 25.8 us
    pallas_call x0 -> x1, Pallas kernels: none -> 120 us  [reaction(): pl.pallas_call(reaction_kernel, out_shape=jax.ShapeDtypeStruct((nx, ny, c...]
    dot_general x14 -> x0, matrix products: 69.5 us -> none  [product(): jnp.einsum('bij,bjn->bin', matrices, values, precision=lax.Precision.HIGH...]
    ppermute x4, starting transfers between devices: 78 us -> 8.94 us  [padded_2(): before = lax.ppermute(last, axis, up)]
    while x60 -> x0, local copies, waits for them, and re-layouts: 39.6 us -> none
    another operation x2 -> x0, loops' own time: 9.35 us -> none  [run_sweeps(): return lax.fori_loop(0, trip_count, sweep_once, jnp.zeros_like(source))]
    ppermute x4, waiting for transfers between devices: 6.81 us -> 15.9 us  [padded_2(): before = lax.ppermute(last, axis, up)]
    reshape x2 -> x0, local copies, waits for them, and re-layouts: 4.72 us -> none  [the longest x1 4.64 us: on_device(): matrices = rate_matrices.reshape(block_count, species_count, species_count)]
    unnamed x10 -> x12, local copies, waits for them, and re-layouts: 0.02 us -> 4.51 us
where the time goes in v1:
time: 184 us
  Pallas kernels  120 us (65%)
  waiting for transfers between devices  25.8 us (14%)
  starting transfers between devices  24 us (13%)
  local copies, waits for them, and re-layouts  7.4 us (4%)
  other arithmetic  6.72 us (4%)
    pallas_call x1, Pallas kernels, reaction(): pl.pallas_call(reaction_kernel, out_shape=jax.ShapeDtypeStruct((nx, ny, c...  120 us
    ppermute x4, waiting for transfers between devices, padded_2(): before = lax.ppermute(last, axis, up)  15.9 us
    ppermute x4, waiting for transfers between devices, padded_2(): after = lax.ppermute(first, axis, down)  9.83 us
    ppermute x4, starting transfers between devices, padded_2(): after = lax.ppermute(first, axis, down)  9.77 us
    ppermute x4, starting transfers between devices, padded_2(): before = lax.ppermute(last, axis, up)  8.94 us
    ppermute x2, starting transfers between devices, from_behind(): return lax.ppermute(array, axis, pairs)  5.32 us
    unnamed x12, local copies, waits for them, and re-layouts  4.51 us
  transfers between devices with their start and end apart: 10, of which 6 were waited for; matrix products, arithmetic and copies ran while one was open for 0% of the time, Pallas kernels for 0%

profile of v1, /device:TPU:12, one launch (start us, length us, event | category | flops | bytes accessed | tf_op | source)
XLA Modules:
  0.0 183.7 jit_solution(1845117865044946938)
XLA Ops:
  0.0 0.0 copy-start
  0.0 1.9 %copy-done = f32[48,8,16,128]{3,2,1,0:T(8,128)S(1)} copy-done((f32[48,8,16,128]{3,2,1,0:T(8,128)S(1)}, f32[48,8,16,128]{3,2,1,0:T(8,128)}, u32[]{:S(2)}) %copy-start) | copy-done | bytes 3145752
  1.9 0.0 copy-start.1
  1.9 1.3 copy-done.1
  3.2 0.0 copy-start.2
  3.2 0.7 copy-done.2
  3.8 0.0 copy-start.3
  3.9 0.7 copy-done.3
  4.5 0.0 copy-start.5
  4.5 0.0 copy-start.4
  4.5 119.5 %reaction.1 = f32[8,16,48,128]{3,2,1,0:T(8,128)S(1)} custom-call(f32[48,8,16,128]{3,2,1,0:T(8,128)S(1)} %copy-done, f32[8,16,2304]{2,1,0:T(8,128)S(1)} %copy-done.1, f32[1,48]{1,0:T(1,128)S(1)} %bitcast.9, s32[8,16]{1,0:T(8,128)S(1)} %copy-done.2), custom_call_target="tpu_custom_call" | custom-call | tf_op jit(solution)/shard_map/reaction/pallas_call | solution.py:82
  124.0 0.1 fusion.13
  124.1 1.9 %collective-permute-start.1 = (f32[48,1,16,128]{3,0,2,1:T(8,128)S(1)}, f32[48,1,16,128]{3,0,2,1:T(8,128)S(1)}, u32[]{:S(2)}, u32[]{:S(2)}) collective-permute-start(f32[48,1,16,128]{3,0,2,1:T(8,128)S(1)} %get-tuple-element.11), channel_id=1, source_target_pairs={{0,2},{2,4},{4,6},{6,8},{8,10},{10,12},{12,14},{14,16},{16,18},{18... | collective-permute-start | bytes 1179656 | tf_op jit(solution)/shard_map/ppermute | solution.py:106
  126.0 3.6 %collective-permute-start.2 = (f32[48,1,16,128]{3,0,2,1:T(8,128)S(1)}, f32[48,1,16,128]{3,0,2,1:T(8,128)S(1)}, u32[]{:S(2)}, u32[]{:S(2)}) collective-permute-start(f32[48,1,16,128]{3,0,2,1:T(8,128)S(1)} %get-tuple-element.12), channel_id=1, source_target_pairs={{2,0},{4,2},{6,4},{8,6},{10,8},{12,10},{14,12},{16,14},{18,16},{20... | collective-permute-start | bytes 1179656 | tf_op jit(solution)/shard_map/ppermute | solution.py:107
  129.7 0.0 copy-done.5
  129.7 3.4 %collective-permute-start.5 = (f32[8,1,128]{2,1,0:T(1,128)S(1)}, f32[8,1,128]{2,1,0:T(1,128)S(1)}, u32[]{:S(2)}, u32[]{:S(2)}) collective-permute-start(f32[8,1,128]{2,1,0:T(1,128)S(1)} %slice.96), channel_id=1, source_target_pairs={{0,1},{2,3},{4,5},{6,7},{8,9},{10,11},{12,13},{14,15},{16,17},{18,... | collective-permute-start | bytes 12296 | tf_op jit(solution)/shard_map/ppermute | solution.py:96
  133.1 0.0 copy-done.4
  133.1 1.9 %collective-permute-start = (f32[1,16,128]{2,1,0:T(8,128)S(1)}, f32[1,16,128]{2,1,0:T(8,128)S(1)}, u32[]{:S(2)}, u32[]{:S(2)}) collective-permute-start(f32[1,16,128]{2,1,0:T(8,128)S(1)} %slice.86), channel_id=1, source_target_pairs={{0,2},{2,4},{4,6},{6,8},{8,10},{10,12},{12,14},{14,16},{16,18},{18... | collective-permute-start | bytes 24584 | tf_op jit(solution)/shard_map/ppermute | solution.py:96
  135.1 0.1 pad.47.clone
  135.1 0.1 pad.36.clone
  135.2 0.0 collective-permute-done.5
  135.2 0.1 maximum_maximum_fusion
  135.3 0.0 collective-permute-done.1
  135.3 1.0 collective-permute-done.2
  136.4 3.5 %collective-permute-start.3 = (f32[48,10,1,128]{3,0,2,1:T(8,128)S(1)}, f32[48,10,1,128]{3,0,2,1:T(8,128)S(1)}, u32[]{:S(2)}, u32[]{:S(2)}) collective-permute-start(f32[48,10,1,128]{3,0,2,1:T(8,128)S(1)} %get-tuple-element.8), channel_id=1, source_target_pairs={{0,1},{2,3},{4,5},{6,7},{8,9},{10,11},{12,13},{14,15},{16,17},{18,... | collective-permute-start | bytes 737288 | tf_op jit(solution)/shard_map/ppermute | solution.py:106
  139.9 1.3 collective-permute-start.4
  141.2 0.0 collective-permute-done
  141.2 0.1 maximum_maximum_fusion.1
  141.3 4.6 %collective-permute-done.3 = f32[48,10,1,128]{3,0,2,1:T(8,128)S(1)} collective-permute-done((f32[48,10,1,128]{3,0,2,1:T(8,128)S(1)}, f32[48,10,1,128]{3,0,2,1:T(8,128)S(1)}, u32[]{:S(2)}, u32[]{:S(2)}) %collective-permute-start.3) | collective-permute-done | bytes 245792 | tf_op jit(solution)/shard_map/ppermute | solution.py:106
  145.9 4.7 %collective-permute-done.4 = f32[48,10,1,128]{3,0,2,1:T(8,128)S(1)} collective-permute-done((f32[48,10,1,128]{3,0,2,1:T(8,128)S(1)}, f32[48,10,1,128]{3,0,2,1:T(8,128)S(1)}, u32[]{:S(2)}, u32[]{:S(2)}) %collective-permute-start.4) | collective-permute-done | bytes 245792 | tf_op jit(solution)/shard_map/ppermute | solution.py:107
  150.6 0.3 pad_maximum_fusion
  150.9 0.8 fusion.3
  151.7 1.5 fusion
  153.2 0.6 fusion.6
  153.9 0.1 fusion.12
  153.9 2.0 %collective-permute-start.6 = (f32[48,1,16,128]{3,0,2,1:T(8,128)S(1)}, f32[48,1,16,128]{3,0,2,1:T(8,128)S(1)}, u32[]{:S(2)}, u32[]{:S(2)}) collective-permute-start(f32[48,1,16,128]{3,0,2,1:T(8,128)S(1)} %get-tuple-element.9), channel_id=1, source_target_pairs={{0,2},{2,4},{4,6},{6,8},{8,10},{10,12},{12,14},{14,16},{16,18},{18... | collective-permute-start | bytes 1179656 | tf_op jit(solution)/shard_map/ppermute | solution.py:106
  156.0 3.5 %collective-permute-start.7 = (f32[48,1,16,128]{3,0,2,1:T(8,128)S(1)}, f32[48,1,16,128]{3,0,2,1:T(8,128)S(1)}, u32[]{:S(2)}, u32[]{:S(2)}) collective-permute-start(f32[48,1,16,128]{3,0,2,1:T(8,128)S(1)} %get-tuple-element.10), channel_id=1, source_target_pairs={{2,0},{4,2},{6,4},{8,6},{10,8},{12,10},{14,12},{16,14},{18,16},{20... | collective-permute-start | bytes 1179656 | tf_op jit(solution)/shard_map/ppermute | solution.py:107
  159.5 7.7 %collective-permute-done.6 = f32[48,1,16,128]{3,0,2,1:T(8,128)S(1)} collective-permute-done((f32[48,1,16,128]{3,0,2,1:T(8,128)S(1)}, f32[48,1,16,128]{3,0,2,1:T(8,128)S(1)}, u32[]{:S(2)}, u32[]{:S(2)}) %collective-permute-start.6) | collective-permute-done | bytes 393248 | tf_op jit(solution)/shard_map/ppermute | solution.py:106
  167.2 0.0 collective-permute-done.7
  167.3 1.5 collective-permute-start.8
  168.8 1.3 collective-permute-start.9
  170.1 3.6 %collective-permute-done.8 = f32[48,10,1,128]{3,0,2,1:T(8,128)S(1)} collective-permute-done((f32[48,10,1,128]{3,0,2,1:T(8,128)S(1)}, f32[48,10,1,128]{3,0,2,1:T(8,128)S(1)}, u32[]{:S(2)}, u32[]{:S(2)}) %collective-permute-start.8) | collective-permute-done | bytes 245792 | tf_op jit(solution)/shard_map/ppermute | solution.py:106
  173.7 4.1 %collective-permute-done.9 = f32[48,10,1,128]{3,0,2,1:T(8,128)S(1)} collective-permute-done((f32[48,10,1,128]{3,0,2,1:T(8,128)S(1)}, f32[48,10,1,128]{3,0,2,1:T(8,128)S(1)}, u32[]{:S(2)}, u32[]{:S(2)}) %collective-permute-start.9) | collective-permute-done | bytes 245792 | tf_op jit(solution)/shard_map/ppermute | solution.py:107
  177.8 0.3 pad_maximum_fusion.1
  178.1 0.8 fusion.2
  178.9 1.5 fusion.1
  180.4 0.6 fusion.4
  181.0 2.6 %copy.7 = f32[48,8,16,128]{3,2,1,0:T(8,128)} copy(f32[48,8,16,128]{3,0,2,1:T(8,128)S(1)} %fusion.4) | data formatting | bytes 6291456 | tf_op jit(solution)/shard_map/sub | solution.py:123
  (6 shorter events, 0.1 us)
Async XLA Ops:
  0.0 1.9 %copy-start = (f32[48,8,16,128]{3,2,1,0:T(8,128)S(1)}, f32[48,8,16,128]{3,2,1,0:T(8,128)}, u32[]{:S(2)}) copy-start(f32[48,8,16,128]{3,2,1,0:T(8,128)} %species_ref.1) | copy-start | bytes 9437188
  1.9 1.3 copy-start.1
  3.2 0.7 copy-start.2
  3.8 0.7 copy-start.3
  4.5 125.2 %copy-start.5 = (f32[8,16,128]{2,1,0:T(8,128)S(1)}, f32[8,16,128]{2,1,0:T(8,128)}, u32[]{:S(2)}) copy-start(f32[8,16,128]{2,1,0:T(8,128)} %param.11) | copy-start | bytes 196612
  4.5 128.6 %copy-start.4 = (f32[8,16,128]{2,1,0:T(8,128)S(1)}, f32[8,16,128]{2,1,0:T(8,128)}, u32[]{:S(2)}) copy-start(f32[8,16,128]{2,1,0:T(8,128)} %param.10) | copy-start | bytes 196612
  124.1 11.2 %collective-permute-start.1 = (f32[48,1,16,128]{3,0,2,1:T(8,128)S(1)}, f32[48,1,16,128]{3,0,2,1:T(8,128)S(1)}, u32[]{:S(2)}, u32[]{:S(2)}) collective-permute-start(f32[48,1,16,128]{3,0,2,1:T(8,128)S(1)} %get-tuple-element.11), channel_id=1, source_target_pairs={{0,2},{2,4},{4,6},{6,8},{8,10},{10,12},{12,14},{14,16},{16,18},{18... | collective-permute-start | bytes 1179656 | tf_op jit(solution)/shard_map/ppermute | solution.py:106
  126.0 10.3 %collective-permute-start.2 = (f32[48,1,16,128]{3,0,2,1:T(8,128)S(1)}, f32[48,1,16,128]{3,0,2,1:T(8,128)S(1)}, u32[]{:S(2)}, u32[]{:S(2)}) collective-permute-start(f32[48,1,16,128]{3,0,2,1:T(8,128)S(1)} %get-tuple-element.12), channel_id=1, source_target_pairs={{2,0},{4,2},{6,4},{8,6},{10,8},{12,10},{14,12},{16,14},{18,16},{20... | collective-permute-start | bytes 1179656 | tf_op jit(solution)/shard_map/ppermute | solution.py:107
  129.7 5.5 %collective-permute-start.5 = (f32[8,1,128]{2,1,0:T(1,128)S(1)}, f32[8,1,128]{2,1,0:T(1,128)S(1)}, u32[]{:S(2)}, u32[]{:S(2)}) collective-permute-start(f32[8,1,128]{2,1,0:T(1,128)S(1)} %slice.96), channel_id=1, source_target_pairs={{0,1},{2,3},{4,5},{6,7},{8,9},{10,11},{12,13},{14,15},{16,17},{18,... | collective-permute-start | bytes 12296 | tf_op jit(solution)/shard_map/ppermute | solution.py:96
  133.1 8.1 %collective-permute-start = (f32[1,16,128]{2,1,0:T(8,128)S(1)}, f32[1,16,128]{2,1,0:T(8,128)S(1)}, u32[]{:S(2)}, u32[]{:S(2)}) collective-permute-start(f32[1,16,128]{2,1,0:T(8,128)S(1)} %slice.86), channel_id=1, source_target_pairs={{0,2},{2,4},{4,6},{6,8},{8,10},{10,12},{12,14},{14,16},{16,18},{18... | collective-permute-start | bytes 24584 | tf_op jit(solution)/shard_map/ppermute | solution.py:96
  136.4 9.5 %collective-permute-start.3 = (f32[48,10,1,128]{3,0,2,1:T(8,128)S(1)}, f32[48,10,1,128]{3,0,2,1:T(8,128)S(1)}, u32[]{:S(2)}, u32[]{:S(2)}) collective-permute-start(f32[48,10,1,128]{3,0,2,1:T(8,128)S(1)} %get-tuple-element.8), channel_id=1, source_target_pairs={{0,1},{2,3},{4,5},{6,7},{8,9},{10,11},{12,13},{14,15},{16,17},{18,... | collective-permute-start | bytes 737288 | tf_op jit(solution)/shard_map/ppermute | solution.py:106
  139.9 10.7 %collective-permute-start.4 = (f32[48,10,1,128]{3,0,2,1:T(8,128)S(1)}, f32[48,10,1,128]{3,0,2,1:T(8,128)S(1)}, u32[]{:S(2)}, u32[]{:S(2)}) collective-permute-start(f32[48,10,1,128]{3,0,2,1:T(8,128)S(1)} %get-tuple-element.7), channel_id=1, source_target_pairs={{1,0},{3,2},{5,4},{7,6},{9,8},{11,10},{13,12},{15,14},{17,16},{19,... | collective-permute-start | bytes 737288 | tf_op jit(solution)/shard_map/ppermute | solution.py:107
  153.9 13.3 %collective-permute-start.6 = (f32[48,1,16,128]{3,0,2,1:T(8,128)S(1)}, f32[48,1,16,128]{3,0,2,1:T(8,128)S(1)}, u32[]{:S(2)}, u32[]{:S(2)}) collective-permute-start(f32[48,1,16,128]{3,0,2,1:T(8,128)S(1)} %get-tuple-element.9), channel_id=1, source_target_pairs={{0,2},{2,4},{4,6},{6,8},{8,10},{10,12},{12,14},{14,16},{16,18},{18... | collective-permute-start | bytes 1179656 | tf_op jit(solution)/shard_map/ppermute | solution.py:106
  156.0 11.3 %collective-permute-start.7 = (f32[48,1,16,128]{3,0,2,1:T(8,128)S(1)}, f32[48,1,16,128]{3,0,2,1:T(8,128)S(1)}, u32[]{:S(2)}, u32[]{:S(2)}) collective-permute-start(f32[48,1,16,128]{3,0,2,1:T(8,128)S(1)} %get-tuple-element.10), channel_id=1, source_target_pairs={{2,0},{4,2},{6,4},{8,6},{10,8},{12,10},{14,12},{16,14},{18,16},{20... | collective-permute-start | bytes 1179656 | tf_op jit(solution)/shard_map/ppermute | solution.py:107
  167.3 6.4 %collective-permute-start.8 = (f32[48,10,1,128]{3,0,2,1:T(8,128)S(1)}, f32[48,10,1,128]{3,0,2,1:T(8,128)S(1)}, u32[]{:S(2)}, u32[]{:S(2)}) collective-permute-start(f32[48,10,1,128]{3,0,2,1:T(8,128)S(1)} %get-tuple-element.6), channel_id=1, source_target_pairs={{0,1},{2,3},{4,5},{6,7},{8,9},{10,11},{12,13},{14,15},{16,17},{18,... | collective-permute-start | bytes 737288 | tf_op jit(solution)/shard_map/ppermute | solution.py:106
  168.8 9.0 %collective-permute-start.9 = (f32[48,10,1,128]{3,0,2,1:T(8,128)S(1)}, f32[48,10,1,128]{3,0,2,1:T(8,128)S(1)}, u32[]{:S(2)}, u32[]{:S(2)}) collective-permute-start(f32[48,10,1,128]{3,0,2,1:T(8,128)S(1)} %get-tuple-element.5), channel_id=1, source_target_pairs={{1,0},{3,2},{5,4},{7,6},{9,8},{11,10},{13,12},{15,14},{17,16},{19,... | collective-permute-start | bytes 737288 | tf_op jit(solution)/shard_map/ppermute | solution.py:107

commit v2 on v1

--- a/solution.py
+++ b/solution.py
@@ -27,29 +27,44 @@
     return jnp.dot(a, b, preferred_element_type=jnp.float32)
 
 
-def react(matrix, v, count, loss, eye):
-    diagonal = jnp.sum(jnp.where(eye, matrix, 0.0), axis=1, keepdims=True)
-    inverse = 1.0 / (1.0 - section_gamma * diagonal)
-    m1 = jnp.where(eye, 0.0, matrix * (section_gamma * inverse))
-    right_1 = right(m1)
-    m2 = mm(left(m1), right_1)
-    left_2 = left(m2)
-    m3 = mm(left_2, right_1)
-    m4 = mm(left_2, right(m2))
-    left_4 = left(m4)
-    m5 = mm(left_4, right_1)
-    p4 = jnp.where(eye, 1.0, 0.0) + m1 + m2 + m3
-    even = jnp.where(count % 2 == 0, 1.0, 0.0)
-    short = p4 + m4 + even * m5
-    full = p4 + mm(left_4, right(short))
-    left_p = left(jnp.where(count > 8, full, short))
-    left_a = left(matrix)
-    r1 = mm(left_a, right(v)) - loss * v * v
-    k1 = mm(left_p, right(r1 * inverse))
-    w = v + k1
-    r2 = mm(left_a, right(w)) - loss * w * w - 2.0 * k1
-    k2 = mm(left_p, right(r2 * inverse))
-    return v + 1.5 * k1 + 0.5 * k2
+def react(matrices, states, counts, loss, eye):
+    def each(f, *lists):
+        return [f(*parts) for parts in zip(*lists)]
+
+    def inverse_of(a):
+        diagonal = jnp.sum(jnp.where(eye, a, 0.0), axis=1, keepdims=True)
+        return 1.0 / (1.0 - section_gamma * diagonal)
+
+    def solve(lefts, sources):
+        return each(mm, lefts, each(lambda r, i: right(r * i), sources, inverse))
+
+    left_a = each(left, matrices)
+    inverse = each(inverse_of, matrices)
+    m1 = each(lambda a, i: jnp.where(eye, 0.0, a * (section_gamma * i)), matrices, inverse)
+    right_1 = each(right, m1)
+    m2 = each(mm, each(left, m1), right_1)
+    av = each(mm, left_a, each(right, states))
+    left_2 = each(left, m2)
+    m3 = each(mm, left_2, right_1)
+    m4 = each(mm, left_2, each(right, m2))
+    r1 = each(lambda p, v: p - loss * v * v, av, states)
+    left_4 = each(left, m4)
+    m5 = each(mm, left_4, right_1)
+    unit = jnp.where(eye, 1.0, 0.0)
+    p4 = each(lambda a, b, c: unit + a + b + c, m1, m2, m3)
+    short = each(
+        lambda p, a, b, n: p + a + jnp.where(n % 2 == 0, 1.0, 0.0) * b, p4, m4, m5, counts
+    )
+    rest = each(mm, left_4, each(right, short))
+    left_p = each(
+        lambda p, q, s, n: left(jnp.where(n > 8, p + q, s)), p4, rest, short, counts
+    )
+    k1 = solve(left_p, r1)
+    w = each(lambda v, k: v + k, states, k1)
+    aw = each(mm, left_a, each(right, w))
+    r2 = each(lambda p, u, k: p - loss * u * u - 2.0 * k, aw, w, k1)
+    k2 = solve(left_p, r2)
+    return each(lambda v, a, b: v + 1.5 * a + 0.5 * b, states, k1, k2)
 
 
 def reaction_kernel(species_ref, rates_ref, loss_ref, sweeps_ref, out_ref, rows_ref):
@@ -69,11 +84,11 @@
             rows_ref[i * 8 : i * 8 + 8, 0:count] = rates_ref[
                 x, pl.ds(first, 8), i * count : (i + 1) * count
             ]
-        for j in range(8):
-            y = first + j
-            matrix = rows_ref[pl.ds(j, count, stride=8), :][:, :count]
-            v = flat[pl.ds(x * ny + y, count, stride=nx * ny), :]
-            out_ref[x, y] = react(matrix, v, sweeps_ref[x, y], loss, eye)
+        matrices = [rows_ref[pl.ds(j, count, stride=8), :][:, :count] for j in range(8)]
+        states = [flat[pl.ds(x * ny + first + j, count, stride=nx * ny), :] for j in range(8)]
+        counts = [sweeps_ref[x, first + j] for j in range(8)]
+        for j, result in enumerate(react(matrices, states, counts, loss, eye)):
+            out_ref[x, first + j] = result
 
 
 def reaction(species, rates, loss, sweeps):

time: 184 us -> 94.1 us (0.51)
  Pallas kernels: 120 us -> 29.5 us
    pallas_call x1, Pallas kernels: 120 us -> 29.5 us  [reaction(): pl.pallas_call(reaction_kernel, out_shape=jax.ShapeDtypeStruct((nx, ny, c...]
where the time goes in v2:
time: 94.1 us; the launch traced here: 93.7 us
  Pallas kernels  29.5 us (31%)
  waiting for transfers between devices  25.8 us (27%)
  starting transfers between devices  24 us (26%)
  local copies, waits for them, and re-layouts  7.4 us (8%)
  other arithmetic  6.72 us (7%)
    pallas_call x1, Pallas kernels, reaction(): pl.pallas_call(reaction_kernel, out_shape=jax.ShapeDtypeStruct((nx, ny, c...  29.5 us
    ppermute x4, waiting for transfers between devices, padded_2(): before = lax.ppermute(last, axis, up)  15.9 us
    ppermute x4, waiting for transfers between devices, padded_2(): after = lax.ppermute(first, axis, down)  9.84 us
    ppermute x4, starting transfers between devices, padded_2(): after = lax.ppermute(first, axis, down)  9.77 us
    ppermute x4, starting transfers between devices, padded_2(): before = lax.ppermute(last, axis, up)  8.94 us
    ppermute x2, starting transfers between devices, from_behind(): return lax.ppermute(array, axis, pairs)  5.31 us
    unnamed x12, local copies, waits for them, and re-layouts  4.51 us
    add x2, other arithmetic, advect(): jnp.maximum(flow_second[:, :-1], 0.0) * concentration[:, :, :-1]  2.96 us
  transfers between devices with their start and end apart: 10, of which 6 were waited for; matrix products, arithmetic and copies ran while one was open for 0% of the time, Pallas kernels for 0%

profile of v2, /device:TPU:12, one launch (start us, length us, event | category | flops | bytes accessed | tf_op | source)
XLA Modules:
  0.0 93.7 jit_solution(16880945604269342400)
XLA Ops:
  0.0 0.0 copy-start
  0.0 1.9 %copy-done = f32[48,8,16,128]{3,2,1,0:T(8,128)S(1)} copy-done((f32[48,8,16,128]{3,2,1,0:T(8,128)S(1)}, f32[48,8,16,128]{3,2,1,0:T(8,128)}, u32[]{:S(2)}) %copy-start) | copy-done | bytes 3145752
  1.9 0.0 copy-start.1
  1.9 1.3 %copy-done.1 = f32[8,16,2304]{2,1,0:T(8,128)S(1)} copy-done((f32[8,16,2304]{2,1,0:T(8,128)S(1)}, f32[8,16,2304]{2,1,0:T(8,128)}, u32[]{:S(2)}) %copy-start.1) | copy-done | bytes 1179672
  3.2 0.0 copy-start.2
  3.2 0.7 copy-done.2
  3.8 0.0 copy-start.3
  3.9 0.7 copy-done.3
  4.5 0.0 copy-start.5
  4.5 0.0 copy-start.4
  4.5 29.5 %reaction.1 = f32[8,16,48,128]{3,2,1,0:T(8,128)S(1)} custom-call(f32[48,8,16,128]{3,2,1,0:T(8,128)S(1)} %copy-done, f32[8,16,2304]{2,1,0:T(8,128)S(1)} %copy-done.1, f32[1,48]{1,0:T(1,128)S(1)} %bitcast.9, s32[8,16]{1,0:T(8,128)S(1)} %copy-done.2), custom_call_target="tpu_custom_call" | custom-call | tf_op jit(solution)/shard_map/reaction/pallas_call | solution.py:97
  34.1 0.1 fusion.13
  34.1 1.9 %collective-permute-start.1 = (f32[48,1,16,128]{3,0,2,1:T(8,128)S(1)}, f32[48,1,16,128]{3,0,2,1:T(8,128)S(1)}, u32[]{:S(2)}, u32[]{:S(2)}) collective-permute-start(f32[48,1,16,128]{3,0,2,1:T(8,128)S(1)} %get-tuple-element.11), channel_id=1, source_target_pairs={{0,2},{2,4},{4,6},{6,8},{8,10},{10,12},{12,14},{14,16},{16,18},{18... | collective-permute-start | bytes 1179656 | tf_op jit(solution)/shard_map/ppermute | solution.py:121
  36.1 3.6 %collective-permute-start.2 = (f32[48,1,16,128]{3,0,2,1:T(8,128)S(1)}, f32[48,1,16,128]{3,0,2,1:T(8,128)S(1)}, u32[]{:S(2)}, u32[]{:S(2)}) collective-permute-start(f32[48,1,16,128]{3,0,2,1:T(8,128)S(1)} %get-tuple-element.12), channel_id=1, source_target_pairs={{2,0},{4,2},{6,4},{8,6},{10,8},{12,10},{14,12},{16,14},{18,16},{20... | collective-permute-start | bytes 1179656 | tf_op jit(solution)/shard_map/ppermute | solution.py:122
  39.7 0.0 copy-done.5
  39.7 3.4 %collective-permute-start.5 = (f32[8,1,128]{2,1,0:T(1,128)S(1)}, f32[8,1,128]{2,1,0:T(1,128)S(1)}, u32[]{:S(2)}, u32[]{:S(2)}) collective-permute-start(f32[8,1,128]{2,1,0:T(1,128)S(1)} %slice.96), channel_id=1, source_target_pairs={{0,1},{2,3},{4,5},{6,7},{8,9},{10,11},{12,13},{14,15},{16,17},{18,... | collective-permute-start | bytes 12296 | tf_op jit(solution)/shard_map/ppermute | solution.py:111
  43.1 0.0 copy-done.4
  43.1 1.9 %collective-permute-start = (f32[1,16,128]{2,1,0:T(8,128)S(1)}, f32[1,16,128]{2,1,0:T(8,128)S(1)}, u32[]{:S(2)}, u32[]{:S(2)}) collective-permute-start(f32[1,16,128]{2,1,0:T(8,128)S(1)} %slice.86), channel_id=1, source_target_pairs={{0,2},{2,4},{4,6},{6,8},{8,10},{10,12},{12,14},{14,16},{16,18},{18... | collective-permute-start | bytes 24584 | tf_op jit(solution)/shard_map/ppermute | solution.py:111
  45.1 0.1 pad.47.clone
  45.2 0.1 pad.36.clone
  45.2 0.0 collective-permute-done.5
  45.2 0.1 maximum_maximum_fusion
  45.3 0.0 collective-permute-done.1
  45.3 1.0 %collective-permute-done.2 = f32[48,1,16,128]{3,0,2,1:T(8,128)S(1)} collective-permute-done((f32[48,1,16,128]{3,0,2,1:T(8,128)S(1)}, f32[48,1,16,128]{3,0,2,1:T(8,128)S(1)}, u32[]{:S(2)}, u32[]{:S(2)}) %collective-permute-start.2) | collective-permute-done | bytes 393248 | tf_op jit(solution)/shard_map/ppermute | solution.py:122
  46.4 3.5 %collective-permute-start.3 = (f32[48,10,1,128]{3,0,2,1:T(8,128)S(1)}, f32[48,10,1,128]{3,0,2,1:T(8,128)S(1)}, u32[]{:S(2)}, u32[]{:S(2)}) collective-permute-start(f32[48,10,1,128]{3,0,2,1:T(8,128)S(1)} %get-tuple-element.8), channel_id=1, source_target_pairs={{0,1},{2,3},{4,5},{6,7},{8,9},{10,11},{12,13},{14,15},{16,17},{18,... | collective-permute-start | bytes 737288 | tf_op jit(solution)/shard_map/ppermute | solution.py:121
  49.9 1.3 %collective-permute-start.4 = (f32[48,10,1,128]{3,0,2,1:T(8,128)S(1)}, f32[48,10,1,128]{3,0,2,1:T(8,128)S(1)}, u32[]{:S(2)}, u32[]{:S(2)}) collective-permute-start(f32[48,10,1,128]{3,0,2,1:T(8,128)S(1)} %get-tuple-element.7), channel_id=1, source_target_pairs={{1,0},{3,2},{5,4},{7,6},{9,8},{11,10},{13,12},{15,14},{17,16},{19,... | collective-permute-start | bytes 737288 | tf_op jit(solution)/shard_map/ppermute | solution.py:122
  51.2 0.0 collective-permute-done
  51.2 0.1 maximum_maximum_fusion.1
  51.3 4.6 %collective-permute-done.3 = f32[48,10,1,128]{3,0,2,1:T(8,128)S(1)} collective-permute-done((f32[48,10,1,128]{3,0,2,1:T(8,128)S(1)}, f32[48,10,1,128]{3,0,2,1:T(8,128)S(1)}, u32[]{:S(2)}, u32[]{:S(2)}) %collective-permute-start.3) | collective-permute-done | bytes 245792 | tf_op jit(solution)/shard_map/ppermute | solution.py:121
  55.9 4.7 %collective-permute-done.4 = f32[48,10,1,128]{3,0,2,1:T(8,128)S(1)} collective-permute-done((f32[48,10,1,128]{3,0,2,1:T(8,128)S(1)}, f32[48,10,1,128]{3,0,2,1:T(8,128)S(1)}, u32[]{:S(2)}, u32[]{:S(2)}) %collective-permute-start.4) | collective-permute-done | bytes 245792 | tf_op jit(solution)/shard_map/ppermute | solution.py:122
  60.6 0.3 pad_maximum_fusion
  60.9 0.8 fusion.3
  61.7 1.5 %fusion = f32[48,10,17,128]{3,0,2,1:T(8,128)S(1)} fusion(f32[48,1,16,128]{3,0,2,1:T(8,128)S(1)} %collective-permute-done.2, f32[48,8,16,128]{3,0,2,1:T(8,128)S(1)} %bitcast.8, f32[48,1,16,128]{3,0,2,1:T(8,128)S(1)} %collective-permute-done.1, f32[48,10,1,128]{3,0,2,1:T(8,128)S(1)} %collective-permute-done.3, ...), kind=kLoop, calls=%fused_computation.3 | loop fusion | flops 9400320 | bytes 8775680 | tf_op jit(solution)/shard_map/add | solution.py:133
  63.3 0.6 fusion.6
  63.9 0.1 fusion.12
  64.0 2.0 %collective-permute-start.6 = (f32[48,1,16,128]{3,0,2,1:T(8,128)S(1)}, f32[48,1,16,128]{3,0,2,1:T(8,128)S(1)}, u32[]{:S(2)}, u32[]{:S(2)}) collective-permute-start(f32[48,1,16,128]{3,0,2,1:T(8,128)S(1)} %get-tuple-element.9), channel_id=1, source_target_pairs={{0,2},{2,4},{4,6},{6,8},{8,10},{10,12},{12,14},{14,16},{16,18},{18... | collective-permute-start | bytes 1179656 | tf_op jit(solution)/shard_map/ppermute | solution.py:121
  66.0 3.5 %collective-permute-start.7 = (f32[48,1,16,128]{3,0,2,1:T(8,128)S(1)}, f32[48,1,16,128]{3,0,2,1:T(8,128)S(1)}, u32[]{:S(2)}, u32[]{:S(2)}) collective-permute-start(f32[48,1,16,128]{3,0,2,1:T(8,128)S(1)} %get-tuple-element.10), channel_id=1, source_target_pairs={{2,0},{4,2},{6,4},{8,6},{10,8},{12,10},{14,12},{16,14},{18,16},{20... | collective-permute-start | bytes 1179656 | tf_op jit(solution)/shard_map/ppermute | solution.py:122
  69.5 7.7 %collective-permute-done.6 = f32[48,1,16,128]{3,0,2,1:T(8,128)S(1)} collective-permute-done((f32[48,1,16,128]{3,0,2,1:T(8,128)S(1)}, f32[48,1,16,128]{3,0,2,1:T(8,128)S(1)}, u32[]{:S(2)}, u32[]{:S(2)}) %collective-permute-start.6) | collective-permute-done | bytes 393248 | tf_op jit(solution)/shard_map/ppermute | solution.py:121
  77.3 0.0 collective-permute-done.7
  77.3 1.5 %collective-permute-start.8 = (f32[48,10,1,128]{3,0,2,1:T(8,128)S(1)}, f32[48,10,1,128]{3,0,2,1:T(8,128)S(1)}, u32[]{:S(2)}, u32[]{:S(2)}) collective-permute-start(f32[48,10,1,128]{3,0,2,1:T(8,128)S(1)} %get-tuple-element.6), channel_id=1, source_target_pairs={{0,1},{2,3},{4,5},{6,7},{8,9},{10,11},{12,13},{14,15},{16,17},{18,... | collective-permute-start | bytes 737288 | tf_op jit(solution)/shard_map/ppermute | solution.py:121
  78.8 1.3 %collective-permute-start.9 = (f32[48,10,1,128]{3,0,2,1:T(8,128)S(1)}, f32[48,10,1,128]{3,0,2,1:T(8,128)S(1)}, u32[]{:S(2)}, u32[]{:S(2)}) collective-permute-start(f32[48,10,1,128]{3,0,2,1:T(8,128)S(1)} %get-tuple-element.5), channel_id=1, source_target_pairs={{1,0},{3,2},{5,4},{7,6},{9,8},{11,10},{13,12},{15,14},{17,16},{19,... | collective-permute-start | bytes 737288 | tf_op jit(solution)/shard_map/ppermute | solution.py:122
  80.1 3.6 %collective-permute-done.8 = f32[48,10,1,128]{3,0,2,1:T(8,128)S(1)} collective-permute-done((f32[48,10,1,128]{3,0,2,1:T(8,128)S(1)}, f32[48,10,1,128]{3,0,2,1:T(8,128)S(1)}, u32[]{:S(2)}, u32[]{:S(2)}) %collective-permute-start.8) | collective-permute-done | bytes 245792 | tf_op jit(solution)/shard_map/ppermute | solution.py:121
  83.7 4.1 %collective-permute-done.9 = f32[48,10,1,128]{3,0,2,1:T(8,128)S(1)} collective-permute-done((f32[48,10,1,128]{3,0,2,1:T(8,128)S(1)}, f32[48,10,1,128]{3,0,2,1:T(8,128)S(1)}, u32[]{:S(2)}, u32[]{:S(2)}) %collective-permute-start.9) | collective-permute-done | bytes 245792 | tf_op jit(solution)/shard_map/ppermute | solution.py:122
  87.8 0.3 pad_maximum_fusion.1
  88.1 0.8 fusion.2
  89.0 1.5 %fusion.1 = f32[48,10,17,128]{3,0,2,1:T(8,128)S(1)} fusion(f32[48,1,16,128]{3,0,2,1:T(8,128)S(1)} %collective-permute-done.7, f32[48,8,16,128]{3,0,2,1:T(8,128)S(1)} %fusion.6, f32[48,1,16,128]{3,0,2,1:T(8,128)S(1)} %collective-permute-done.6, f32[48,10,1,128]{3,0,2,1:T(8,128)S(1)} %collective-permute-done.8, ...), kind=kLoop, calls=%fused_computation.6 | loop fusion | flops 9400320 | bytes 8775680 | tf_op jit(solution)/shard_map/add | solution.py:133
  90.4 0.6 fusion.4
  91.1 2.6 %copy.7 = f32[48,8,16,128]{3,2,1,0:T(8,128)} copy(f32[48,8,16,128]{3,0,2,1:T(8,128)S(1)} %fusion.4) | data formatting | bytes 6291456 | tf_op jit(solution)/shard_map/sub | solution.py:138
  (6 shorter events, 0.1 us)
Async XLA Ops:
  0.0 1.9 %copy-start = (f32[48,8,16,128]{3,2,1,0:T(8,128)S(1)}, f32[48,8,16,128]{3,2,1,0:T(8,128)}, u32[]{:S(2)}) copy-start(f32[48,8,16,128]{3,2,1,0:T(8,128)} %species_ref.1) | copy-start | bytes 9437188
  1.9 1.3 %copy-start.1 = (f32[8,16,2304]{2,1,0:T(8,128)S(1)}, f32[8,16,2304]{2,1,0:T(8,128)}, u32[]{:S(2)}) copy-start(f32[8,16,2304]{2,1,0:T(8,128)} %rates_ref.1) | copy-start | bytes 3538948
  3.2 0.7 copy-start.2
  3.8 0.7 copy-start.3
  4.5 35.2 %copy-start.5 = (f32[8,16,128]{2,1,0:T(8,128)S(1)}, f32[8,16,128]{2,1,0:T(8,128)}, u32[]{:S(2)}) copy-start(f32[8,16,128]{2,1,0:T(8,128)} %param.11) | copy-start | bytes 196612
  4.5 38.6 %copy-start.4 = (f32[8,16,128]{2,1,0:T(8,128)S(1)}, f32[8,16,128]{2,1,0:T(8,128)}, u32[]{:S(2)}) copy-start(f32[8,16,128]{2,1,0:T(8,128)} %param.10) | copy-start | bytes 196612
  34.1 11.2 %collective-permute-start.1 = (f32[48,1,16,128]{3,0,2,1:T(8,128)S(1)}, f32[48,1,16,128]{3,0,2,1:T(8,128)S(1)}, u32[]{:S(2)}, u32[]{:S(2)}) collective-permute-start(f32[48,1,16,128]{3,0,2,1:T(8,128)S(1)} %get-tuple-element.11), channel_id=1, source_target_pairs={{0,2},{2,4},{4,6},{6,8},{8,10},{10,12},{12,14},{14,16},{16,18},{18... | collective-permute-start | bytes 1179656 | tf_op jit(solution)/shard_map/ppermute | solution.py:121
  36.1 10.3 %collective-permute-start.2 = (f32[48,1,16,128]{3,0,2,1:T(8,128)S(1)}, f32[48,1,16,128]{3,0,2,1:T(8,128)S(1)}, u32[]{:S(2)}, u32[]{:S(2)}) collective-permute-start(f32[48,1,16,128]{3,0,2,1:T(8,128)S(1)} %get-tuple-element.12), channel_id=1, source_target_pairs={{2,0},{4,2},{6,4},{8,6},{10,8},{12,10},{14,12},{16,14},{18,16},{20... | collective-permute-start | bytes 1179656 | tf_op jit(solution)/shard_map/ppermute | solution.py:122
  39.7 5.5 %collective-permute-start.5 = (f32[8,1,128]{2,1,0:T(1,128)S(1)}, f32[8,1,128]{2,1,0:T(1,128)S(1)}, u32[]{:S(2)}, u32[]{:S(2)}) collective-permute-start(f32[8,1,128]{2,1,0:T(1,128)S(1)} %slice.96), channel_id=1, source_target_pairs={{0,1},{2,3},{4,5},{6,7},{8,9},{10,11},{12,13},{14,15},{16,17},{18,... | collective-permute-start | bytes 12296 | tf_op jit(solution)/shard_map/ppermute | solution.py:111
  43.1 8.1 %collective-permute-start = (f32[1,16,128]{2,1,0:T(8,128)S(1)}, f32[1,16,128]{2,1,0:T(8,128)S(1)}, u32[]{:S(2)}, u32[]{:S(2)}) collective-permute-start(f32[1,16,128]{2,1,0:T(8,128)S(1)} %slice.86), channel_id=1, source_target_pairs={{0,2},{2,4},{4,6},{6,8},{8,10},{10,12},{12,14},{14,16},{16,18},{18... | collective-permute-start | bytes 24584 | tf_op jit(solution)/shard_map/ppermute | solution.py:111
  46.4 9.5 %collective-permute-start.3 = (f32[48,10,1,128]{3,0,2,1:T(8,128)S(1)}, f32[48,10,1,128]{3,0,2,1:T(8,128)S(1)}, u32[]{:S(2)}, u32[]{:S(2)}) collective-permute-start(f32[48,10,1,128]{3,0,2,1:T(8,128)S(1)} %get-tuple-element.8), channel_id=1, source_target_pairs={{0,1},{2,3},{4,5},{6,7},{8,9},{10,11},{12,13},{14,15},{16,17},{18,... | collective-permute-start | bytes 737288 | tf_op jit(solution)/shard_map/ppermute | solution.py:121
  49.9 10.7 %collective-permute-start.4 = (f32[48,10,1,128]{3,0,2,1:T(8,128)S(1)}, f32[48,10,1,128]{3,0,2,1:T(8,128)S(1)}, u32[]{:S(2)}, u32[]{:S(2)}) collective-permute-start(f32[48,10,1,128]{3,0,2,1:T(8,128)S(1)} %get-tuple-element.7), channel_id=1, source_target_pairs={{1,0},{3,2},{5,4},{7,6},{9,8},{11,10},{13,12},{15,14},{17,16},{19,... | collective-permute-start | bytes 737288 | tf_op jit(solution)/shard_map/ppermute | solution.py:122
  64.0 13.3 %collective-permute-start.6 = (f32[48,1,16,128]{3,0,2,1:T(8,128)S(1)}, f32[48,1,16,128]{3,0,2,1:T(8,128)S(1)}, u32[]{:S(2)}, u32[]{:S(2)}) collective-permute-start(f32[48,1,16,128]{3,0,2,1:T(8,128)S(1)} %get-tuple-element.9), channel_id=1, source_target_pairs={{0,2},{2,4},{4,6},{6,8},{8,10},{10,12},{12,14},{14,16},{16,18},{18... | collective-permute-start | bytes 1179656 | tf_op jit(solution)/shard_map/ppermute | solution.py:121
  66.0 11.3 %collective-permute-start.7 = (f32[48,1,16,128]{3,0,2,1:T(8,128)S(1)}, f32[48,1,16,128]{3,0,2,1:T(8,128)S(1)}, u32[]{:S(2)}, u32[]{:S(2)}) collective-permute-start(f32[48,1,16,128]{3,0,2,1:T(8,128)S(1)} %get-tuple-element.10), channel_id=1, source_target_pairs={{2,0},{4,2},{6,4},{8,6},{10,8},{12,10},{14,12},{16,14},{18,16},{20... | collective-permute-start | bytes 1179656 | tf_op jit(solution)/shard_map/ppermute | solution.py:122
  77.3 6.4 %collective-permute-start.8 = (f32[48,10,1,128]{3,0,2,1:T(8,128)S(1)}, f32[48,10,1,128]{3,0,2,1:T(8,128)S(1)}, u32[]{:S(2)}, u32[]{:S(2)}) collective-permute-start(f32[48,10,1,128]{3,0,2,1:T(8,128)S(1)} %get-tuple-element.6), channel_id=1, source_target_pairs={{0,1},{2,3},{4,5},{6,7},{8,9},{10,11},{12,13},{14,15},{16,17},{18,... | collective-permute-start | bytes 737288 | tf_op jit(solution)/shard_map/ppermute | solution.py:121
  78.8 9.0 %collective-permute-start.9 = (f32[48,10,1,128]{3,0,2,1:T(8,128)S(1)}, f32[48,10,1,128]{3,0,2,1:T(8,128)S(1)}, u32[]{:S(2)}, u32[]{:S(2)}) collective-permute-start(f32[48,10,1,128]{3,0,2,1:T(8,128)S(1)} %get-tuple-element.5), channel_id=1, source_target_pairs={{1,0},{3,2},{5,4},{7,6},{9,8},{11,10},{13,12},{15,14},{17,16},{19,... | collective-permute-start | bytes 737288 | tf_op jit(solution)/shard_map/ppermute | solution.py:122

commit v3 on v2

v3 whole, which is shorter than its diff:
```python
import functools

import jax
import jax.numpy as jnp
from jax import lax
from jax.experimental import pallas as pl
from jax.experimental.pallas import tpu as pltpu
from jax.sharding import PartitionSpec as P

section_gamma = 1.0 + 0.5**0.5


def halves(x):
    hi = x.astype(jnp.bfloat16)
    return hi, (x - hi.astype(jnp.float32)).astype(jnp.bfloat16)


def left(x):
    hi, lo = halves(x)
    return jnp.concatenate([hi, lo, hi], axis=1)


def right(x):
    hi, lo = halves(x)
    return jnp.concatenate([hi, hi, lo], axis=0)


def mm(a, b):
    return jnp.dot(a, b, preferred_element_type=jnp.float32)


def react(matrices, states, counts, loss, eye):
    def each(f, *lists):
        return [f(*parts) for parts in zip(*lists)]

    def inverse_of(a):
        diagonal = jnp.sum(jnp.where(eye, a, 0.0), axis=1, keepdims=True)
        return 1.0 / (1.0 - section_gamma * diagonal)

    def solve(lefts, sources):
        return each(mm, lefts, each(lambda r, i: right(r * i), sources, inverse))

    left_a = each(left, matrices)
    inverse = each(inverse_of, matrices)
    m1 = each(lambda a, i: jnp.where(eye, 0.0, a * (section_gamma * i)), matrices, inverse)
    right_1 = each(right, m1)
    m2 = each(mm, each(left, m1), right_1)
    av = each(mm, left_a, each(right, states))
    left_2 = each(left, m2)
    m3 = each(mm, left_2, right_1)
    m4 = each(mm, left_2, each(right, m2))
    r1 = each(lambda p, v: p - loss * v * v, av, states)
    left_4 = each(left, m4)
    m5 = each(mm, left_4, right_1)
    unit = jnp.where(eye, 1.0, 0.0)
    p4 = each(lambda a, b, c: unit + a + b + c, m1, m2, m3)
    short = each(
        lambda p, a, b, n: p + a + jnp.where(n % 2 == 0, 1.0, 0.0) * b, p4, m4, m5, counts
    )
    rest = each(mm, left_4, each(right, short))
    left_p = each(
        lambda p, q, s, n: left(jnp.where(n > 8, p + q, s)), p4, rest, short, counts
    )
    k1 = solve(left_p, r1)
    w = each(lambda v, k: v + k, states, k1)
    aw = each(mm, left_a, each(right, w))
    r2 = each(lambda p, u, k: p - loss * u * u - 2.0 * k, aw, w, k1)
    k2 = solve(left_p, r2)
    return each(lambda v, a, b: v + 1.5 * a + 0.5 * b, states, k1, k2)


ways = tuple((dx, dy) for dx in (-1, 0, 1) for dy in (-1, 0, 1) if (dx, dy) != (0, 0))


def span(way, size, corner):
    if way == 0:
        return slice(2, 2 + size), slice(2, 2 + size)
    width = 1 if corner else 2
    if way < 0:
        return slice(2, 2 + width), slice(2 + size, 2 + size + width)
    return slice(2 + size - width, 2 + size), slice(2 - width, 2)


def slab_kernel(
    extent,
    species_ref,
    rates_ref,
    loss_ref,
    sweeps_ref,
    flow_rows_ref,
    flow_columns_ref,
    out_ref,
    cells,
    moved,
    flows,
    rates,
    flow_send,
    flow_recv,
    cell_send,
    cell_recv,
):
    count, nx, ny, depth = species_ref.shape
    here = (lax.axis_index("gx"), lax.axis_index("gy"))

    def there(way):
        found = None
        for part, position, size in zip(way, here, extent):
            if part:
                inside = position > 0 if part < 0 else position < size - 1
                found = inside if found is None else found & inside
        return found

    def halo(buffer, send, recv, index):
        way = ways[index]
        corner = way[0] != 0 and way[1] != 0
        rows, rows_to = span(way[0], nx, corner)
        columns, columns_to = span(way[1], ny, corner)
        return pltpu.make_async_remote_copy(
            src_ref=buffer.at[rows, columns],
            dst_ref=buffer.at[rows_to, columns_to],
            send_sem=send.at[index],
            recv_sem=recv.at[index],
            device_id=(here[0] + way[0], here[1] + way[1]),
            device_id_type=pl.DeviceIdType.MESH,
        )

    def start(buffer, send, recv, chosen):
        for index, way in enumerate(ways):
            if chosen(way):

                @pl.when(there(way))
                def _():
                    halo(buffer, send, recv, index).start()

    def finish(buffer, send, recv):
        for index, way in enumerate(ways):

            @pl.when(there(way))
            def _():
                halo(buffer, send, recv, index).wait_send()

            @pl.when(there((-way[0], -way[1])))
            def _():
                halo(buffer, send, recv, index).wait_recv()

    empty = jnp.zeros((ny + 4, count, depth), jnp.float32)
    for x in (0, 1, nx + 2, nx + 3):
        cells[x] = empty
    for y in (0, 1, ny + 2, ny + 3):
        cells[:, y] = jnp.zeros((nx + 4, count, depth), jnp.float32)
    flows[...] = jnp.zeros_like(flows)

    barrier = pltpu.get_barrier_semaphore()
    for way in ways:

        @pl.when(there(way))
        def _():
            pl.semaphore_signal(
                barrier,
                inc=1,
                device_id=(here[0] + way[0], here[1] + way[1]),
                device_id_type=pl.DeviceIdType.MESH,
            )

    beside = [
        1 + jnp.where(position > 0, 1, 0) + jnp.where(position < size - 1, 1, 0)
        for position, size in zip(here, extent)
    ]
    pl.semaphore_wait(barrier, beside[0] * beside[1] - 1)

    flow_lines = flows.reshape((nx + 4) * (ny + 4) * 8, depth)
    for x in range(nx):
        line = ((x + 2) * (ny + 4) + 2) * 8
        flow_lines[pl.ds(line, ny, stride=8), :] = flow_rows_ref[x]
        flow_lines[pl.ds(line + 1, ny, stride=8), :] = flow_columns_ref[x]
    start(flows, flow_send, flow_recv, lambda way: True)

    flat = species_ref.reshape(count * nx * ny, depth)
    octets = ny // 8
    eye = lax.broadcasted_iota(jnp.int32, (count, count), 0) == lax.broadcasted_iota(
        jnp.int32, (count, count), 1
    )
    loss = jnp.sum(jnp.where(eye, loss_ref[...], 0.0), axis=1, keepdims=True)

    @pl.loop(0, nx * octets)
    def _(octet):
        x = octet // octets
        first = pl.multiple_of((octet % octets) * 8, 8)
        base = pl.multiple_of(octet * (count * 8), 8)
        for i in range(count):
            rates[pl.ds(base + i * 8, 8), 0:count] = rates_ref[
                x, pl.ds(first, 8), i * count : (i + 1) * count
            ]

    def columns_of(groups, place):
        @pl.loop(0, groups)
        def _(group):
            places = [place(group * 8 + j) for j in range(8)]
            matrices = [
                rates[
                    pl.ds((x * octets + y // 8) * (count * 8) + y % 8, count, stride=8), :
                ][:, :count]
                for x, y in places
            ]
            states = [flat[pl.ds(x * ny + y, count, stride=nx * ny), :] for x, y in places]
            counts = [sweeps_ref[x, y] for x, y in places]
            for (x, y), result in zip(places, react(matrices, states, counts, loss, eye)):
                cells[x + 2, y + 2] = result

    inner = ny - 4
    columns_of(ny // 4, lambda i: (i // ny, i % ny))
    start(cells, cell_send, cell_recv, lambda way: way[0] < 0)
    columns_of(ny // 4, lambda i: (nx - 2 + i // ny, i % ny))
    start(cells, cell_send, cell_recv, lambda way: way[0] > 0)
    columns_of((nx - 4) // 2, lambda i: (2 + i // 4, i % 4 + i % 4 // 2 * inner))
    start(cells, cell_send, cell_recv, lambda way: way[0] == 0)
    columns_of((nx - 4) * inner // 8, lambda i: (2 + i // inner, 2 + i % inner))
    finish(flows, flow_send, flow_recv)
    finish(cells, cell_send, cell_recv)

    def substep(c, x, y):
        down = flows[x, y, 0:1, :]
        up = flows[x - 1, y, 0:1, :]
        after = flows[x, y, 1:2, :]
        before = flows[x, y - 1, 1:2, :]
        from_down = -jnp.minimum(down, 0.0)
        from_up = jnp.maximum(up, 0.0)
        from_after = -jnp.minimum(after, 0.0)
        from_before = jnp.maximum(before, 0.0)
        kept = (
            1.0
            - (jnp.maximum(down, 0.0) - jnp.minimum(up, 0.0))
            - (jnp.maximum(after, 0.0) - jnp.minimum(before, 0.0))
        )
        return (
            kept * c[x, y]
            + from_down * c[x + 1, y]
            + from_up * c[x - 1, y]
            + from_after * c[x, y + 1]
            + from_before * c[x, y - 1]
        )

    @pl.loop(1, nx + 3)
    def _(x):
        @pl.loop(0, (ny + 2) // 6)
        def _(part):
            for j in range(6):
                moved[x, part * 6 + j + 1] = substep(cells, x, part * 6 + j + 1)

    @pl.when(here[0] == extent[0] - 1)
    def _():
        moved[nx + 2] = empty

    @pl.when(here[1] == extent[1] - 1)
    def _():
        moved[:, ny + 2] = jnp.zeros((nx + 4, count, depth), jnp.float32)

    @pl.loop(0, nx)
    def _(x):
        @pl.loop(0, ny // 8)
        def _(part):
            for j in range(8):
                y = part * 8 + j
                out_ref[x, y] = substep(moved, x + 2, y + 2)


def on_device(extent, species, rate_matrices, loss_rates, sweeps, flow_rows, flow_columns):
    count, nx, ny, depth = species.shape
    vmem = pl.BlockSpec(memory_space=pltpu.VMEM)
    padded = pltpu.VMEM((nx + 4, ny + 4, count, depth), jnp.float32)
    transported = pl.pallas_call(
        functools.partial(slab_kernel, extent),
        out_shape=jax.ShapeDtypeStruct((nx, ny, count, depth), jnp.float32),
        in_specs=[vmem, vmem, vmem, pl.BlockSpec(memory_space=pltpu.SMEM), vmem, vmem],
        out_specs=vmem,
        scratch_shapes=[
            padded,
            padded,
            pltpu.VMEM((nx + 4, ny + 4, 8, depth), jnp.float32),
            pltpu.VMEM((nx * ny * count, 128), jnp.float32),
        ]
        + [pltpu.SemaphoreType.DMA((len(ways),))] * 4,
        compiler_params=pltpu.CompilerParams(
            collective_id=0, has_side_effects=True, vmem_limit_bytes=48 * 2**20
        ),
        name="slab",
    )(species, rate_matrices, loss_rates.reshape(1, count), sweeps, flow_rows, flow_columns)
    return jnp.transpose(transported, (2, 0, 1, 3))


def solution(mesh):
    placed = (
        P(None, "gx", "gy", None),
        P("gx", "gy", None),
        P(),
        P("gx", "gy"),
        P("gx", "gy", None),
        P("gx", "gy", None),
    )
    extent = (mesh.shape["gx"], mesh.shape["gy"])
    return jax.shard_map(
        functools.partial(on_device, extent), mesh=mesh, in_specs=placed, out_specs=P(None, "gx", "gy", None), check_vma=False
    )
```

time: 94.1 us -> 47.3 us (0.50)
  the two profiles are of different devices: /device:TPU:12 before, /device:TPU:1 now
where the time goes in v3:
time: 47.3 us; the launch traced here: 47 us
  Pallas kernels  40.1 us (85%)
  local copies, waits for them, and re-layouts  6.92 us (15%)
    pallas_call x1, Pallas kernels, on_device(): pl.pallas_call(functools.partial(slab_kernel, extent), out_shape=jax.Shap...  40.1 us
    unnamed x10, local copies, waits for them, and re-layouts  4.29 us
    transpose x1, local copies, waits for them, and re-layouts, on_device(): return jnp.transpose(transported, (2, 0, 1, 3))  2.63 us

profile of v3, /device:TPU:1, one launch (start us, length us, event | category | flops | bytes accessed | tf_op | source)
XLA Modules:
  0.0 47.0 jit_solution(8584779727245394975)
XLA Ops:
  0.0 0.0 copy-start
  0.0 1.3 %copy-done = f32[8,16,2304]{2,1,0:T(8,128)S(1)} copy-done((f32[8,16,2304]{2,1,0:T(8,128)S(1)}, f32[8,16,2304]{2,1,0:T(8,128)}, u32[]{:S(2)}) %copy-start) | copy-done | bytes 1179672
  1.3 0.0 copy-start.1
  1.3 0.8 %copy-done.1 = f32[8,16,128]{2,1,0:T(8,128)S(1)} copy-done((f32[8,16,128]{2,1,0:T(8,128)S(1)}, f32[8,16,128]{2,1,0:T(8,128)}, u32[]{:S(2)}) %copy-start.1) | copy-done | bytes 65560
  2.1 0.0 copy-start.2
  2.1 0.8 %copy-done.2 = f32[8,16,128]{2,1,0:T(8,128)S(1)} copy-done((f32[8,16,128]{2,1,0:T(8,128)S(1)}, f32[8,16,128]{2,1,0:T(8,128)}, u32[]{:S(2)}) %copy-start.2) | copy-done | bytes 65560
  3.0 0.0 copy-start.3
  3.0 0.7 %copy-done.3 = s32[8,16]{1,0:T(8,128)S(1)} copy-done((s32[8,16]{1,0:T(8,128)S(1)}, s32[8,16]{1,0:T(8,128)}, u32[]{:S(2)}) %copy-start.3) | copy-done | bytes 536
  3.6 0.0 copy-start.4
  3.6 0.7 %copy-done.4 = f32[48]{0:T(128)S(1)} copy-done((f32[48]{0:T(128)S(1)}, f32[48]{0:T(128)}, u32[]{:S(2)}) %copy-start.4) | copy-done | bytes 216
  4.3 40.1 %slab.1 = f32[8,16,48,128]{3,2,1,0:T(8,128)S(1)} custom-call(f32[48,8,16,128]{3,2,1,0:T(8,128)} %species_ref.1, f32[8,16,2304]{2,1,0:T(8,128)S(1)} %copy-done, f32[1,48]{1,0:T(1,128)S(1)} %bitcast.3, s32[8,16]{1,0:T(8,128)S(1)} %copy-done.3, f32[8,16,128]{2,1,0:T(8,128)S(1)} %copy-done.1, f32[8,16,128]{2,1,0:T(8,128)S(1)} %copy-done.2), custom_call_target="tpu_custom_call" | custom-call | tf_op jit(solution)/shard_map/slab/pallas_call | solution.py:271
  44.4 2.6 %copy.7 = f32[48,8,16,128]{3,2,1,0:T(8,128)} copy(f32[48,8,16,128]{3,0,2,1:T(8,128)S(1)} %bitcast.2) | data formatting | bytes 6291456 | tf_op jit(solution)/shard_map/transpose | solution.py:288
Async XLA Ops:
  0.0 1.3 %copy-start = (f32[8,16,2304]{2,1,0:T(8,128)S(1)}, f32[8,16,2304]{2,1,0:T(8,128)}, u32[]{:S(2)}) copy-start(f32[8,16,2304]{2,1,0:T(8,128)} %rates_ref.1) | copy-start | bytes 3538948
  1.3 0.8 %copy-start.1 = (f32[8,16,128]{2,1,0:T(8,128)S(1)}, f32[8,16,128]{2,1,0:T(8,128)}, u32[]{:S(2)}) copy-start(f32[8,16,128]{2,1,0:T(8,128)} %flow_rows_ref.1) | copy-start | bytes 196612
  2.1 0.8 %copy-start.2 = (f32[8,16,128]{2,1,0:T(8,128)S(1)}, f32[8,16,128]{2,1,0:T(8,128)}, u32[]{:S(2)}) copy-start(f32[8,16,128]{2,1,0:T(8,128)} %flow_columns_ref.1) | copy-start | bytes 196612
  3.0 0.7 %copy-start.3 = (s32[8,16]{1,0:T(8,128)S(1)}, s32[8,16]{1,0:T(8,128)}, u32[]{:S(2)}) copy-start(s32[8,16]{1,0:T(8,128)} %sweeps_ref.1) | copy-start | bytes 1540
  3.6 0.7 %copy-start.4 = (f32[48]{0:T(128)S(1)}, f32[48]{0:T(128)}, u32[]{:S(2)}) copy-start(f32[48]{0:T(128)} %param.8) | copy-start | bytes 580

commit v4 on v3

--- a/solution.py
+++ b/solution.py
@@ -83,13 +83,19 @@
 
 def slab_kernel(
     extent,
+    species_hbm,
+    rates_hbm,
+    loss_ref,
+    sweeps_hbm,
+    flow_rows_hbm,
+    flow_columns_hbm,
+    out_ref,
     species_ref,
     rates_ref,
-    loss_ref,
     sweeps_ref,
     flow_rows_ref,
     flow_columns_ref,
-    out_ref,
+    fetch,
     cells,
     moved,
     flows,
@@ -100,6 +106,20 @@
     cell_recv,
 ):
     count, nx, ny, depth = species_ref.shape
+    fetches = [
+        pltpu.make_async_copy(source, target, fetch.at[k])
+        for k, (source, target) in enumerate(
+            [
+                (flow_rows_hbm, flow_rows_ref),
+                (flow_columns_hbm, flow_columns_ref),
+                (rates_hbm, rates_ref),
+                (sweeps_hbm, sweeps_ref),
+                (species_hbm, species_ref),
+            ]
+        )
+    ]
+    for copy in fetches:
+        copy.start()
     here = (lax.axis_index("gx"), lax.axis_index("gy"))
 
     def there(way):
@@ -168,6 +188,8 @@
     ]
     pl.semaphore_wait(barrier, beside[0] * beside[1] - 1)
 
+    fetches[0].wait()
+    fetches[1].wait()
     flow_lines = flows.reshape((nx + 4) * (ny + 4) * 8, depth)
     for x in range(nx):
         line = ((x + 2) * (ny + 4) + 2) * 8
@@ -181,6 +203,8 @@
         jnp.int32, (count, count), 1
     )
     loss = jnp.sum(jnp.where(eye, loss_ref[...], 0.0), axis=1, keepdims=True)
+
+    fetches[2].wait()
 
     @pl.loop(0, nx * octets)
     def _(octet):
@@ -195,7 +219,7 @@
     def columns_of(groups, place):
         @pl.loop(0, groups)
         def _(group):
-            places = [place(group * 8 + j) for j in range(8)]
+            places = [place(group * 16 + j) for j in range(16)]
             matrices = [
                 rates[
                     pl.ds((x * octets + y // 8) * (count * 8) + y % 8, count, stride=8), :
@@ -207,14 +231,16 @@
             for (x, y), result in zip(places, react(matrices, states, counts, loss, eye)):
                 cells[x + 2, y + 2] = result
 
+    fetches[3].wait()
+    fetches[4].wait()
     inner = ny - 4
-    columns_of(ny // 4, lambda i: (i // ny, i % ny))
+    columns_of(ny // 8, lambda i: (i // ny, i % ny))
     start(cells, cell_send, cell_recv, lambda way: way[0] < 0)
-    columns_of(ny // 4, lambda i: (nx - 2 + i // ny, i % ny))
+    columns_of(ny // 8, lambda i: (nx - 2 + i // ny, i % ny))
     start(cells, cell_send, cell_recv, lambda way: way[0] > 0)
-    columns_of((nx - 4) // 2, lambda i: (2 + i // 4, i % 4 + i % 4 // 2 * inner))
+    columns_of((nx - 4) // 4, lambda i: (2 + i // 4, i % 4 + i % 4 // 2 * inner))
     start(cells, cell_send, cell_recv, lambda way: way[0] == 0)
-    columns_of((nx - 4) * inner // 8, lambda i: (2 + i // inner, 2 + i % inner))
+    columns_of((nx - 4) * inner // 16, lambda i: (2 + i // inner, 2 + i % inner))
     finish(flows, flow_send, flow_recv)
     finish(cells, cell_send, cell_recv)
 
@@ -267,13 +293,20 @@
 def on_device(extent, species, rate_matrices, loss_rates, sweeps, flow_rows, flow_columns):
     count, nx, ny, depth = species.shape
     vmem = pl.BlockSpec(memory_space=pltpu.VMEM)
+    hbm = pl.BlockSpec(memory_space=pltpu.HBM)
     padded = pltpu.VMEM((nx + 4, ny + 4, count, depth), jnp.float32)
     transported = pl.pallas_call(
         functools.partial(slab_kernel, extent),
         out_shape=jax.ShapeDtypeStruct((nx, ny, count, depth), jnp.float32),
-        in_specs=[vmem, vmem, vmem, pl.BlockSpec(memory_space=pltpu.SMEM), vmem, vmem],
+        in_specs=[hbm, hbm, vmem, hbm, hbm, hbm],
         out_specs=vmem,
         scratch_shapes=[
+            pltpu.VMEM(species.shape, jnp.float32),
+            pltpu.VMEM(rate_matrices.shape, jnp.float32),
+            pltpu.SMEM(sweeps.shape, jnp.int32),
+            pltpu.VMEM(flow_rows.shape, jnp.float32),
+            pltpu.VMEM(flow_columns.shape, jnp.float32),
+            pltpu.SemaphoreType.DMA((5,)),
             padded,
             padded,
             pltpu.VMEM((nx + 4, ny + 4, 8, depth), jnp.float32),
@@ -281,7 +314,7 @@
         ]
         + [pltpu.SemaphoreType.DMA((len(ways),))] * 4,
         compiler_params=pltpu.CompilerParams(
-            collective_id=0, has_side_effects=True, vmem_limit_bytes=48 * 2**20
+            collective_id=0, has_side_effects=True, vmem_limit_bytes=60 * 2**20
         ),
         name="slab",
     )(species, rate_matrices, loss_rates.reshape(1, count), sweeps, flow_rows, flow_columns)

time: 47.3 us -> 40.6 us (0.86)
  the two profiles are of different devices: /device:TPU:1 before, /device:TPU:12 now
where the time goes in v4:
time: 40.6 us; the launch traced here: 40.3 us
  Pallas kernels  35.7 us (88%)
  local copies, waits for them, and re-layouts  4.57 us (11%)
    pallas_call x1, Pallas kernels, on_device(): pl.pallas_call(functools.partial(slab_kernel, extent), out_shape=jax.Shap...  35.7 us
    transpose x1, local copies, waits for them, and re-layouts, on_device(): return jnp.transpose(transported, (2, 0, 1, 3))  4.57 us

profile of v4, /device:TPU:12, one launch (start us, length us, event | category | flops | bytes accessed | tf_op | source)
XLA Modules:
  0.0 40.3 jit_solution(3513793400613127997)
XLA Ops:
  0.0 35.7 %slab.1 = f32[8,16,48,128]{3,2,1,0:T(8,128)} custom-call(f32[48,8,16,128]{3,2,1,0:T(8,128)} %species_hbm.1, f32[8,16,2304]{2,1,0:T(8,128)} %rates_hbm.1, f32[1,48]{1,0:T(1,128)} %bitcast.3, s32[8,16]{1,0:T(8,128)} %sweeps_hbm.1, f32[8,16,128]{2,1,0:T(8,128)} %flow_rows_hbm.1, f32[8,16,128]{2,1,0:T(8,128)} %flow_columns_hbm.1), custom_call_target="tpu_custom_call" | custom-call | tf_op jit(solution)/shard_map/slab/pallas_call | solution.py:298
  35.7 4.6 %copy.7 = f32[48,8,16,128]{3,2,1,0:T(8,128)} copy(f32[48,8,16,128]{3,0,2,1:T(8,128)} %bitcast.2) | data formatting | bytes 6291456 | tf_op jit(solution)/shard_map/transpose | solution.py:321

commit v5 on v4

--- a/solution.py
+++ b/solution.py
@@ -197,6 +197,7 @@
         flow_lines[pl.ds(line + 1, ny, stride=8), :] = flow_columns_ref[x]
     start(flows, flow_send, flow_recv, lambda way: True)
 
+    out_lines = out_ref.reshape(count * nx * ny, depth)
     flat = species_ref.reshape(count * nx * ny, depth)
     octets = ny // 8
     eye = lax.broadcasted_iota(jnp.int32, (count, count), 0) == lax.broadcasted_iota(
@@ -287,7 +288,9 @@
         def _(part):
             for j in range(8):
                 y = part * 8 + j
-                out_ref[x, y] = substep(moved, x + 2, y + 2)
+                out_lines[pl.ds(x * ny + y, count, stride=nx * ny), :] = substep(
+                    moved, x + 2, y + 2
+                )
 
 
 def on_device(extent, species, rate_matrices, loss_rates, sweeps, flow_rows, flow_columns):
@@ -295,9 +298,9 @@
     vmem = pl.BlockSpec(memory_space=pltpu.VMEM)
     hbm = pl.BlockSpec(memory_space=pltpu.HBM)
     padded = pltpu.VMEM((nx + 4, ny + 4, count, depth), jnp.float32)
-    transported = pl.pallas_call(
+    return pl.pallas_call(
         functools.partial(slab_kernel, extent),
-        out_shape=jax.ShapeDtypeStruct((nx, ny, count, depth), jnp.float32),
+        out_shape=jax.ShapeDtypeStruct(species.shape, jnp.float32),
         in_specs=[hbm, hbm, vmem, hbm, hbm, hbm],
         out_specs=vmem,
         scratch_shapes=[
@@ -318,7 +321,6 @@
         ),
         name="slab",
     )(species, rate_matrices, loss_rates.reshape(1, count), sweeps, flow_rows, flow_columns)
-    return jnp.transpose(transported, (2, 0, 1, 3))
 
 
 def solution(mesh):

time: 40.6 us -> 42.5 us (1.047)
  Pallas kernels: 35.7 us -> 38.3 us
  local copies, waits for them, and re-layouts: 4.57 us -> 3.91 us
    transpose x1 -> x0, local copies, waits for them, and re-layouts: 4.57 us -> none  [on_device(): return jnp.transpose(transported, (2, 0, 1, 3))]
    unnamed x0 -> x1, local copies, waits for them, and re-layouts: none -> 3.91 us
    pallas_call x1, Pallas kernels: 35.7 us -> 38.3 us  [on_device(): pl.pallas_call(functools.partial(slab_kernel, extent), out_shape=jax.Shap...]
where the time goes in v5:
time: 42.5 us; the launch traced here: 42.2 us
  Pallas kernels  38.3 us (90%)
  local copies, waits for them, and re-layouts  3.91 us (9%)
    pallas_call x1, Pallas kernels, on_device(): pl.pallas_call(functools.partial(slab_kernel, extent), out_shape=jax.Shap...  38.3 us
    unnamed x1, local copies, waits for them, and re-layouts  3.91 us

profile of v5, /device:TPU:12, one launch (start us, length us, event | category | flops | bytes accessed | tf_op | source)
XLA Modules:
  0.0 42.2 jit_solution(9627716212233275746)
XLA Ops:
  0.0 38.3 %slab.1 = f32[48,8,16,128]{3,2,1,0:T(8,128)} custom-call(f32[48,8,16,128]{3,2,1,0:T(8,128)} %species_hbm.1, f32[8,16,2304]{2,1,0:T(8,128)} %rates_hbm.1, f32[1,48]{1,0:T(1,128)} %bitcast.1, s32[8,16]{1,0:T(8,128)} %sweeps_hbm.1, f32[8,16,128]{2,1,0:T(8,128)} %flow_rows_hbm.1, f32[8,16,128]{2,1,0:T(8,128)} %flow_columns_hbm.1), custom_call_target="tpu_custom_call" | custom-call | tf_op jit(solution)/shard_map/slab/pallas_call | solution.py:301
  38.3 3.9 %copy.8 = f32[48,8,16,128]{3,2,1,0:T(8,128)} copy(f32[48,8,16,128]{3,2,1,0:T(8,128)} %slab.1) | data formatting | bytes 6291456
